TPU v7x, 128 devices: a whole 4x4x4 slice. The times are simulated.
128 devices in a mesh: rep: 16 (over x, y_lo, core), grp: 8 (over y_hi, z).
Axes of the slice: x: 4, y: 4 (y_hi: 2, y_lo: 2; y = y_hi * 2 + y_lo), z: 4, core: 2. Of those that a mesh axis runs over, the one named last changes fastest.
Arguments:
- tokens: bfloat16 [16, 1536, 1024], P('rep', 'grp'), may hold values from -6 to 6
- span_order: int32 [16, 16], P('rep'), may hold values from 0 to 15, each once within a row
- query_weight: bfloat16 [1024, 1024], P('grp'), may hold values from -0.1875 to 0.1875
- key_weight: bfloat16 [1024, 512], P('grp'), may hold values from -0.1875 to 0.1875
- value_weight: bfloat16 [1024, 512], P('grp'), may hold values from -0.1875 to 0.1875
- out_weight: bfloat16 [1024, 1024], P('grp'), may hold values from -1.5 to 1.5
- gate_weight: bfloat16 [1024, 4608], P('grp'), may hold values from -0.1875 to 0.1875
- up_weight: bfloat16 [1024, 4608], P('grp'), may hold values from -0.1875 to 0.1875
- down_weight: bfloat16 [4608, 1024], P('grp'), may hold values from -0.09375 to 0.09375
- attn_gain: bfloat16 [1024], P('grp'), may hold values from 0.25 to 1.75
- ffn_gain: bfloat16 [1024], P('grp'), may hold values from 0.25 to 1.75
- query_gain: bfloat16 [64], P('grp'), may hold values from 0.25 to 1.75
- key_gain: bfloat16 [64], P('grp'), may hold values from 0.25 to 1.75
- cotangent: bfloat16 [16, 1536, 1024], P('rep', 'grp'), may hold values from -6 to 6
Outputs:
- outputs: bfloat16 [16, 1536, 1024], P('rep', 'grp')
- input_grad: float32 [16, 1536, 1024], P('rep', 'grp')
- query_grad: float32 [1024, 1024], P('grp')
- key_grad: float32 [1024, 512], P('grp')
- value_grad: float32 [1024, 512], P('grp')
- out_grad: float32 [1024, 1024], P('grp')
- gate_grad: float32 [1024, 4608], P('grp')
- up_grad: float32 [1024, 4608], P('grp')
- down_grad: float32 [4608, 1024], P('grp')
- attn_gain_grad: float32 [1024], P('grp')
- ffn_gain_grad: float32 [1024], P('grp')
- query_gain_grad: float32 [64], P('grp')
- key_gain_grad: float32 [64], P('grp')
Inputs may be any that keep to these rules, and one draw needn't show every extreme that they name: `span_order`: each row is a permutation: the stored blocks of a sequence hold all 16 blocks of positions once each.
All inputs are finite; a program needn't handle non-finite values.
Results may differ from a plain program's by a relative error of at most 0.034.
Values may be sent and summed in bfloat16 or wider, within the bound.
No kernel may reach another device: no remote copies, remote signals or barrier semaphores. Data moves between devices by JAX's collectives and lax.ppermute only.
A program may use at most 192 MiB of HBM per device.

v0:
```python
import functools
import math

import jax
import jax.numpy as jnp
from jax import lax
from jax.experimental import pallas as pl
from jax.experimental.pallas import tpu as pltpu
from jax.sharding import PartitionSpec as P

H = 16
KVH = 8
HD = 64
CH = 96
SEQ = 1536
SPANS = 16
TILE = 256
TILES = SEQ // TILE
EPS = 1e-05
THETA = 1000000.0
AXES = ("rep", "grp")
F32 = jnp.float32
BF16 = jnp.bfloat16
VMEM_LIMIT = 48 * 1024 * 1024


def coords(i):
    rep, grp = divmod(i, 8)
    return rep // 4, (rep // 2) % 2, rep % 2, grp // 4, grp % 4


def index_of(x, ylo, core, yhi, z):
    return ((x * 2 + ylo) * 2 + core) * 8 + yhi * 4 + z


def permutation(move):
    return [(i, index_of(*move(*coords(i)))) for i in range(128)]


X_UP = permutation(lambda x, a, c, b, z: ((x + 1) % 4, a, c, b, z))
X_DOWN = permutation(lambda x, a, c, b, z: ((x - 1) % 4, a, c, b, z))
Y_SWAP = permutation(lambda x, a, c, b, z: (x, 1 - a, c, b, z))
CORE_SWAP = permutation(lambda x, a, c, b, z: (x, a, 1 - c, b, z))


def send(value, perm):
    return lax.ppermute(value, AXES, perm)


def exchange_grp(value):
    return lax.all_to_all(value, "grp", 0, 0)


def to_grp(piece):
    return jnp.broadcast_to(piece[None], (8,) + piece.shape)


def x_gather(own):
    half = own.shape[0] // 2
    left = send(own, X_UP)
    right = send(own, X_DOWN)
    far_a = send(left[:half], X_UP)
    far_b = send(right[half:], X_DOWN)
    return own, left, right, jnp.concatenate([far_a, far_b], axis=0)


def x_reduce(parts):
    own, left, right, far = parts
    half = own.shape[0] // 2
    far = far.astype(BF16)
    got_a = send(far[:half], X_UP)
    got_b = send(far[half:], X_DOWN)
    right = jnp.concatenate([right[:half] + got_a.astype(F32), right[half:]], axis=0)
    left = jnp.concatenate([left[:half], left[half:] + got_b.astype(F32)], axis=0)
    from_left = send(right.astype(BF16), X_UP)
    from_right = send(left.astype(BF16), X_DOWN)
    return own + from_left.astype(F32) + from_right.astype(F32)


def tie(*values):
    return lax.optimization_barrier(values)


def rms_norm(values, gain):
    return values * lax.rsqrt(jnp.mean(values * values, axis=-1, keepdims=True) + EPS) * gain


def rotary():
    ladder = jnp.arange(HD // 2, dtype=F32) * (2.0 / HD)
    freq = jnp.exp(-math.log(THETA) * ladder)
    angle = jnp.arange(SEQ, dtype=F32)[None, :] * freq[:, None]
    return jnp.cos(angle), jnp.sin(angle)


def mask_tile():
    key = lax.broadcasted_iota(jnp.int32, (TILE, 2 * TILE), 0)
    query = lax.broadcasted_iota(jnp.int32, (TILE, 2 * TILE), 1)
    return key <= jnp.where(query >= TILE, query - TILE, query)


def dot(a, b):
    return jnp.dot(a, b, preferred_element_type=F32)


def span_of(i):
    return slice(i * TILE, (i + 1) * TILE)


def block_start(order_ref, c):
    return pl.multiple_of(order_ref[c] * CH, CH)


def forward_kernel(
    order_ref, tokens_ref, weight_ref, attn_gain_ref, head_gain_ref, cos_ref, sin_ref,
    mixed_ref, input_ref, cols_ref, rows_ref, lin_t_ref, out_t_ref, log_ref,
    lin_rows, keys, mixed_rows,
):
    for j in range(4):
        part = slice(j * 4 * CH, (j + 1) * 4 * CH)
        x = tokens_ref[part, :].astype(F32)
        r = lax.rsqrt(jnp.mean(x * x, axis=1, keepdims=True) + EPS)
        normed = (x * r * attn_gain_ref[...]).astype(BF16)
        input_ref[part, :] = normed
        lin = dot(normed, weight_ref[...])
        for k in range(4):
            lin_rows[pl.ds(block_start(order_ref, 4 * j + k), CH), :] = lin[k * CH : (k + 1) * CH, :]
    for i in range(TILES):
        span = span_of(i)
        lin_t = lin_rows[span, :].T
        lin_t_ref[:, span] = lin_t[0:192, :]
        cosine, sine = cos_ref[:, span], sin_ref[:, span]
        parts = []
        for h, kind, scale in ((0, 0, HD ** (-0.5)), (1, 0, HD ** (-0.5)), (2, 1, 1.0)):
            u = lin_t[h * 64 : (h + 1) * 64, :]
            r = lax.rsqrt(jnp.mean(u * u, axis=0, keepdims=True) + EPS)
            n = u * r * head_gain_ref[:, kind : kind + 1]
            low, high = n[:32, :], n[32:, :]
            parts += [(low * cosine - high * sine) * scale, (high * cosine + low * sine) * scale]
        both = jnp.concatenate(parts + [lin_t[192:256, :]], axis=0)
        cols_ref[:, span] = both.astype(BF16)
        flat = both.T.astype(BF16)
        rows_ref[span, :] = flat
        keys[span, :] = flat[:, 128:192]
    mask = mask_tile()
    for i in range(TILES):
        span = span_of(i)
        query = jnp.concatenate([cols_ref[0:64, span], cols_ref[64:128, span]], axis=1)
        total = jnp.zeros((64, 2 * TILE), F32)
        weight = jnp.zeros((1, 2 * TILE), F32)
        for c in range(i + 1):
            key_span = span_of(c)
            expo = jnp.exp(dot(keys[key_span, :], query))
            if c == i:
                expo = jnp.where(mask, expo, 0.0)
            weight = weight + jnp.sum(expo, axis=0, keepdims=True)
            total = total + dot(cols_ref[192:256, key_span], expo.astype(BF16))
        total = total / weight
        logs = jnp.log(weight)
        out_t_ref[0:64, span] = total[:, :TILE]
        out_t_ref[64:128, span] = total[:, TILE:]
        log_ref[0:1, span] = logs[:, :TILE]
        log_ref[1:2, span] = logs[:, TILE:]
        mixed_rows[span, :] = (
            jnp.concatenate([total[:, :TILE], total[:, TILE:]], axis=0).T.astype(BF16)
        )
    log_ref[2:8, :] = jnp.zeros((6, SEQ), F32)
    for c in range(SPANS):
        mixed_ref[c * CH : (c + 1) * CH, :] = mixed_rows[pl.ds(block_start(order_ref, c), CH), :]


VMEM_SPEC = pl.BlockSpec(memory_space=pltpu.VMEM)
SMEM_SPEC = pl.BlockSpec(memory_space=pltpu.SMEM)


def attend_forward(order, tokens, weight, attn_gain, head_gain, cosine, sine):
    return pl.pallas_call(
        forward_kernel,
        out_shape=(
            jax.ShapeDtypeStruct((SEQ, 128), BF16),
            jax.ShapeDtypeStruct((SEQ, 1024), BF16),
            jax.ShapeDtypeStruct((256, SEQ), BF16),
            jax.ShapeDtypeStruct((SEQ, 256), BF16),
            jax.ShapeDtypeStruct((192, SEQ), F32),
            jax.ShapeDtypeStruct((128, SEQ), F32),
            jax.ShapeDtypeStruct((8, SEQ), F32),
        ),
        in_specs=[SMEM_SPEC] + [VMEM_SPEC] * 6,
        out_specs=(VMEM_SPEC,) * 7,
        scratch_shapes=[
            pltpu.VMEM((SEQ, 256), F32),
            pltpu.VMEM((SEQ, 64), BF16),
            pltpu.VMEM((SEQ, 128), BF16),
        ],
        compiler_params=pltpu.CompilerParams(vmem_limit_bytes=VMEM_LIMIT),
        cost_estimate=pl.CostEstimate(
            flops=6 * 10**9, bytes_accessed=14 * 10**6, transcendentals=3 * 10**6
        ),
        name="attend_forward",
    )(order, tokens, weight, attn_gain, head_gain, cosine, sine)


def backward_kernel(
    order_ref, cols_ref, rows_ref, grad_ref, out_t_ref, log_ref, lin_t_ref, head_gain_ref,
    cos_ref, sin_ref, result_ref, gain_ref,
    grad_rows, grad_cols, keys, values, grad_keys, grad_values, grad_query, result_rows,
):
    for c in range(SPANS):
        grad_rows[pl.ds(block_start(order_ref, c), CH), :] = grad_ref[c * CH : (c + 1) * CH, :]
    for i in range(TILES):
        span = span_of(i)
        grad_cols[:, span] = grad_rows[span, :].astype(F32).T.astype(BF16)
        keys[span, :] = rows_ref[span, 128:192]
        values[span, :] = rows_ref[span, 192:256]
    grad_keys[...] = jnp.zeros_like(grad_keys)
    grad_values[...] = jnp.zeros_like(grad_values)
    mask = mask_tile()
    scale = HD ** (-0.5)
    for i in range(TILES):
        span = span_of(i)
        query = jnp.concatenate([cols_ref[0:64, span], cols_ref[64:128, span]], axis=1)
        grad = jnp.concatenate([grad_cols[0:64, span], grad_cols[64:128, span]], axis=1)
        query_rows = jnp.concatenate([rows_ref[span, 0:64], rows_ref[span, 64:128]], axis=0)
        grad_tile = jnp.concatenate([grad_rows[span, 0:64], grad_rows[span, 64:128]], axis=0)
        logs = jnp.concatenate([log_ref[0:1, span], log_ref[1:2, span]], axis=1)
        out_t = jnp.concatenate([out_t_ref[0:64, span], out_t_ref[64:128, span]], axis=1)
        inner = jnp.sum(out_t * grad.astype(F32), axis=0, keepdims=True)
        total = jnp.zeros((64, 2 * TILE), F32)
        for c in range(i + 1):
            key_span = span_of(c)
            attend = jnp.exp(dot(keys[key_span, :], query) - logs)
            if c == i:
                attend = jnp.where(mask, attend, 0.0)
            grad_values[key_span, :] += dot(attend.astype(BF16), grad_tile)
            grad_attend = dot(values[key_span, :], grad)
            grad_scores = (attend * (grad_attend - inner)).astype(BF16)
            grad_keys[key_span, :] += dot(grad_scores, query_rows)
            total = total + dot(cols_ref[128:192, key_span], grad_scores)
        total = total * scale
        grad_query[0:64, span] = total[:, :TILE]
        grad_query[64:128, span] = total[:, TILE:]
    sums = [jnp.zeros((64, TILE), F32), jnp.zeros((64, TILE), F32)]
    for i in range(TILES):
        span = span_of(i)
        cosine, sine = cos_ref[:, span], sin_ref[:, span]
        grads = (grad_query[0:64, span], grad_query[64:128, span], grad_keys[span, :].T)
        parts = []
        for h, kind in ((0, 0), (1, 0), (2, 1)):
            low, high = grads[h][:32, :], grads[h][32:, :]
            g = jnp.concatenate([low * cosine + high * sine, high * cosine - low * sine], axis=0)
            u = lin_t_ref[h * 64 : (h + 1) * 64, span]
            r = lax.rsqrt(jnp.mean(u * u, axis=0, keepdims=True) + EPS)
            wg = g * head_gain_ref[:, kind : kind + 1]
            mean = jnp.mean(u * wg, axis=0, keepdims=True)
            parts.append(wg * r - u * (r * r * r * mean))
            sums[kind] = sums[kind] + g * u * r
        flat = jnp.concatenate(parts, axis=0).T
        result_rows[span, :] = jnp.concatenate([flat, grad_values[span, :]], axis=1).astype(BF16)
    for kind in range(2):
        gain_ref[:, kind * 128 : (kind + 1) * 128] = jnp.broadcast_to(
            jnp.sum(sums[kind], axis=1, keepdims=True), (64, 128)
        )
    for c in range(SPANS):
        result_ref[c * CH : (c + 1) * CH, :] = result_rows[pl.ds(block_start(order_ref, c), CH), :]


def attend_backward(order, cols, rows, grad, out_t, logs, lin_t, head_gain, cosine, sine):
    return pl.pallas_call(
        backward_kernel,
        out_shape=(
            jax.ShapeDtypeStruct((SEQ, 256), BF16),
            jax.ShapeDtypeStruct((64, 256), F32),
        ),
        in_specs=[SMEM_SPEC] + [VMEM_SPEC] * 9,
        out_specs=(VMEM_SPEC,) * 2,
        scratch_shapes=[
            pltpu.VMEM((SEQ, 128), BF16),
            pltpu.VMEM((128, SEQ), BF16),
            pltpu.VMEM((SEQ, 64), BF16),
            pltpu.VMEM((SEQ, 64), BF16),
            pltpu.VMEM((SEQ, 64), F32),
            pltpu.VMEM((SEQ, 64), F32),
            pltpu.VMEM((128, SEQ), F32),
            pltpu.VMEM((SEQ, 256), BF16),
        ],
        compiler_params=pltpu.CompilerParams(vmem_limit_bytes=VMEM_LIMIT),
        cost_estimate=pl.CostEstimate(
            flops=10 * 10**9, bytes_accessed=8 * 10**6, transcendentals=3 * 10**6
        ),
        name="attend_backward",
    )(order, cols, rows, grad, out_t, logs, lin_t, head_gain, cosine, sine)


def spread_kernel(index_ref, mine_ref, other_ref, down_mine_ref, down_other_ref, gate_ref, up_ref, down_ref):
    core = index_ref[4]
    for x in range(4):
        for source, down_source, place in (
            (mine_ref, down_mine_ref, core),
            (other_ref, down_other_ref, 1 - core),
        ):
            block = source[index_ref[x]].astype(F32)
            rows = pl.ds(pl.multiple_of(place * 64, 64), 64)
            for k, target in enumerate((gate_ref, up_ref)):
                for g in range(8):
                    start = g * 576 + x * 144
                    target[rows, start : start + 144] = block[
                        :, k * 1152 + g * 144 : k * 1152 + (g + 1) * 144
                    ]
            down_rows = pl.ds(pl.multiple_of(x * 144 + place * 72, 8), 72)
            down_ref[down_rows, :] = down_source[index_ref[x]].astype(F32)


def spread_slices(index, mine, other, down_mine, down_other):
    return pl.pallas_call(
        spread_kernel,
        out_shape=(
            jax.ShapeDtypeStruct((128, 4608), F32),
            jax.ShapeDtypeStruct((128, 4608), F32),
            jax.ShapeDtypeStruct((576, 1024), F32),
        ),
        in_specs=[SMEM_SPEC] + [VMEM_SPEC] * 4,
        out_specs=(VMEM_SPEC,) * 3,
        compiler_params=pltpu.CompilerParams(vmem_limit_bytes=VMEM_LIMIT),
        cost_estimate=pl.CostEstimate(flops=10**7, bytes_accessed=10**7, transcendentals=0),
        name="spread_slices",
    )(index, mine, other, down_mine, down_other)


def swiglu(gate_in, up_in):
    return jax.nn.silu(gate_in) * up_in


def per_device(
    tokens, span_order, query_weight, key_weight, value_weight, out_weight,
    gate_weight, up_weight, down_weight, attn_gain, ffn_gain, query_gain, key_gain, cotangent,
):
    rep = lax.axis_index("rep")
    place = lax.axis_index("grp")
    xpos, core = rep // 4, rep % 2
    rows = tokens.shape[1]
    order_row = span_order[0]

    def core_half(matrix):
        half = matrix.shape[0] // 2
        return lax.dynamic_slice_in_dim(matrix, core * half, half, 0)

    def both_cores(mine):
        other = send(mine, CORE_SWAP)
        picked = lax.broadcasted_iota(jnp.int32, (1, 2, 1, 1), 1) == core
        return jnp.where(picked, mine[:, None], other[:, None]).reshape(-1, mine.shape[-1])

    grouped = jnp.concatenate(
        [
            query_weight.reshape(128, KVH, 128),
            key_weight.reshape(128, KVH, HD),
            value_weight.reshape(128, KVH, HD),
        ],
        axis=2,
    )
    gain_rows = jnp.concatenate(
        [
            jnp.concatenate([attn_gain, ffn_gain])[None],
            jnp.concatenate([query_gain, key_gain, jnp.zeros((240,), BF16)])[None],
            jnp.zeros((14, 256), BF16),
        ],
        axis=0,
    )
    got = exchange_grp(
        jnp.concatenate(
            [grouped.transpose(1, 0, 2), jnp.broadcast_to(gain_rows[None], (8, 16, 256))], axis=1
        )
    )
    all_tokens = lax.all_gather(tokens[0], "grp", axis=0, tiled=True)
    def x_columns(matrix):
        cut = matrix.reshape(128, 8, 4, 144)
        return lax.dynamic_index_in_dim(cut, xpos, 2, keepdims=False).reshape(128, 1152)

    gate_up_piece = core_half(jnp.concatenate([x_columns(gate_weight), x_columns(up_weight)], axis=1))
    down_piece = core_half(
        lax.dynamic_index_in_dim(down_weight.reshape(4, 144, 1024), xpos, 0, keepdims=False)
    )
    out_sent, got = tie(to_grp(core_half(out_weight)), got)
    out_half_weight = exchange_grp(out_sent)
    gate_up_sent, down_sent, qkv_sent, out_half_weight = tie(
        to_grp(gate_up_piece),
        to_grp(down_piece),
        to_grp(core_half(grouped.reshape(128, 2048))),
        out_half_weight,
    )
    down_half = exchange_grp(down_sent)

    cot = jnp.concatenate(x_gather(cotangent[0]), axis=0)

    head_weight = got[:, :128].reshape(1024, 256)
    attn_scale = got[:, 128, :128].reshape(1024).astype(F32)
    ffn_scale = got[:, 128, 128:].reshape(1024).astype(F32)
    head_gain = jnp.stack(
        [got[:, 129, 0:8].reshape(HD), got[:, 129, 8:16].reshape(HD)], axis=1
    ).astype(F32)
    x_in = tokens[0].astype(F32)
    cosine, sine = rotary()
    mixed_heads, input_attn, cols, rows_sorted, lin_t, out_t, logs = attend_forward(
        order_row, all_tokens, head_weight, attn_scale[None], head_gain, cosine, sine
    )
    mixed_heads, out_full, cot, down_half = tie(
        mixed_heads, both_cores(out_half_weight), cot, down_half
    )
    mixed = exchange_grp(mixed_heads.reshape(8, rows, 128))
    mixed, gate_up_sent = tie(mixed, gate_up_sent)
    gate_up_half = exchange_grp(gate_up_sent)
    mixed = mixed.transpose(1, 0, 2).reshape(rows, 1024)
    x_mid = x_in + dot(mixed, out_full)

    input_ffn_own = rms_norm(x_mid, ffn_scale).astype(BF16)
    input_ffn = jnp.concatenate(x_gather(input_ffn_own), axis=0)
    down_full = both_cores(down_half)
    qkv_sent, gate_up_half, input_ffn = tie(qkv_sent, gate_up_half, input_ffn)
    qkv_half = exchange_grp(qkv_sent)
    gate_up_full = both_cores(gate_up_half)

    def core_sum(full, half):
        low = full.astype(BF16).reshape(8, 2, half, full.shape[-1])
        mine = lax.dynamic_index_in_dim(low, core, 1, keepdims=False)
        theirs = lax.dynamic_index_in_dim(low, 1 - core, 1, keepdims=False)
        return (mine.astype(F32) + send(theirs, CORE_SWAP).astype(F32)).astype(BF16)

    def y_sum(value):
        return (value.astype(F32) + send(value, Y_SWAP).astype(F32)).astype(BF16)

    def total(value):
        return jnp.sum(value.astype(F32), axis=0).astype(BF16)

    gate_up = dot(input_ffn, gate_up_full)
    gate, up_value = gate_up[:, :1152], gate_up[:, 1152:]
    hidden_exact, pull_swiglu = jax.vjp(swiglu, gate, up_value)
    hidden = hidden_exact.astype(BF16)
    down_grad = jnp.einsum("tf,td->fd", hidden, cot, preferred_element_type=F32)
    down_sent = core_sum(down_grad, 72)
    grad_hidden = jnp.einsum("td,fd->tf", cot, down_full, preferred_element_type=F32)
    grad_gate, grad_up = pull_swiglu(grad_hidden)
    grad_gate_up = jnp.concatenate([grad_gate.astype(BF16), grad_up.astype(BF16)], axis=1)
    grad_gate_up, down_sent, qkv_half = tie(grad_gate_up, down_sent, qkv_half)
    down_got = exchange_grp(down_sent)
    gate_up_grad = jnp.einsum("td,tf->df", input_ffn, grad_gate_up, preferred_element_type=F32)
    gate_up_sent = core_sum(gate_up_grad, 64)
    grad_input_part = jnp.einsum(
        "tf,df->td", grad_gate_up, gate_up_full, preferred_element_type=F32
    )
    grad_input_part, gate_up_sent, down_got = tie(grad_input_part, gate_up_sent, down_got)
    gate_up_got = exchange_grp(gate_up_sent)
    grad_input_ffn = x_reduce(grad_input_part.reshape(4, rows, 1024))
    grad_input_ffn, gate_up_got = tie(grad_input_ffn, gate_up_got)
    down_part = dot(hidden, down_full)

    _, pull_ffn_norm = jax.vjp(rms_norm, x_mid, ffn_scale)
    grad_mid_norm, ffn_gain_grad = pull_ffn_norm(grad_input_ffn)
    grad_mid = cotangent[0].astype(F32) + grad_mid_norm
    grad_attn = grad_mid.astype(BF16)
    grad_mixed = jnp.einsum(
        "td,fd->tf", grad_attn, out_full, preferred_element_type=F32
    ).astype(BF16)
    grad_sent, grad_attn, gate_up_got, down_got = tie(
        grad_mixed.reshape(rows, 8, 128).transpose(1, 0, 2), grad_attn, gate_up_got, down_got
    )
    grad_heads = exchange_grp(grad_sent)
    out_grad = jnp.einsum("tf,td->fd", mixed, grad_attn, preferred_element_type=F32)
    gate_up_sum = y_sum(total(gate_up_got))
    down_sum = y_sum(total(down_got))
    out_sent = core_sum(out_grad, 64)
    grad_heads, out_sent, gate_up_sum, down_sum = tie(
        grad_heads, out_sent, gate_up_sum, down_sum
    )
    out_got = exchange_grp(out_sent)
    gate_up_parts = x_gather(gate_up_sum)
    down_parts = x_gather(down_sum)
    grad_lin, head_gain_grad = attend_backward(
        order_row, cols, rows_sorted, grad_heads.reshape(SEQ, 128), out_t, logs, lin_t,
        head_gain, cosine, sine,
    )
    qkv_grad = jnp.einsum("td,tf->df", input_attn, grad_lin, preferred_element_type=F32)
    grad_lin, out_got, down_part = tie(grad_lin, out_got, down_part)
    outputs = (x_mid + x_reduce(down_part.reshape(4, rows, 1024))).astype(BF16)[None]
    attn_gain_part = jnp.sum(qkv_grad * head_weight.astype(F32), axis=1) / attn_scale
    gain_parts = jnp.concatenate(
        [
            jnp.concatenate(
                [attn_gain_part.reshape(8, 1, 128), ffn_gain_grad.reshape(8, 1, 128)], axis=2
            ),
            jnp.concatenate(
                [
                    head_gain_grad[:, 0].reshape(8, 1, 8),
                    head_gain_grad[:, 128].reshape(8, 1, 8),
                    jnp.zeros((8, 1, 240), F32),
                ],
                axis=2,
            ),
            jnp.zeros((8, 14, 256), F32),
        ],
        axis=1,
    )
    packed = exchange_grp(grad_lin.reshape(8, rows, 256))
    qkv_sent = jnp.concatenate(
        [qkv_grad.astype(BF16).reshape(8, 128, 256), gain_parts.astype(BF16)], axis=1
    )
    qkv_sent, packed = tie(qkv_sent, packed)
    qkv_got = exchange_grp(qkv_sent)
    qkv_got, gate_up_parts, down_parts = tie(qkv_got, gate_up_parts, down_parts)
    grad_packed = packed.transpose(1, 0, 2)
    qkv_rows = qkv_got[:, :128]
    out_sum = jnp.sum(out_got.astype(F32), axis=0).astype(BF16)
    qkv_full = both_cores(qkv_half)
    grad_input_attn = jnp.einsum(
        "tf,df->td", grad_packed.reshape(rows, 2048), qkv_full, preferred_element_type=F32
    )
    _, pull_attn_norm = jax.vjp(lambda v: rms_norm(v, attn_scale), x_in)
    (grad_in_norm,) = pull_attn_norm(grad_input_attn)
    input_grad = (grad_mid + grad_in_norm)[None]

    gain_got = jnp.sum(qkv_got[:, 128:].astype(F32), axis=0)
    gain_owned = jnp.stack(
        [
            gain_got[0, :128],
            gain_got[0, 128:],
            jnp.pad(gain_got[1, 0:8], (0, 120)),
            jnp.pad(gain_got[1, 8:16], (0, 120)),
        ]
    )
    gain_columns = jnp.pad(gain_owned.T, ((0, 0), (0, 252))).astype(BF16)

    own_half = lax.dynamic_update_slice(jnp.zeros((128, 1024), BF16), out_sum, (core * 64, 0))
    attn_rows = jnp.concatenate(
        [qkv_rows.reshape(8, 16, 8, 256).transpose(1, 0, 2, 3).reshape(16, 64, 256)]
        + [own_half[:, k * 256 : (k + 1) * 256].reshape(16, 8, 256) for k in range(4)]
        + [gain_columns.reshape(16, 8, 256)],
        axis=1,
    )
    attn_part = jnp.sum(lax.all_to_all(attn_rows, "rep", 0, 0).astype(F32), axis=0).astype(BF16)
    attn_all = lax.all_to_all(
        jnp.broadcast_to(attn_part[None], (16, 104, 256)), "rep", 0, 0
    )
    heads_all = attn_all[:, :64].reshape(16, 8, 8, 256)

    def by_head(start, stop):
        width = stop - start
        cut = heads_all[:, :, :, start:stop].transpose(0, 2, 1, 3)
        return cut.reshape(128, 8 * width).astype(F32)

    out_all = jnp.concatenate(
        [attn_all[:, 64 + 8 * k : 72 + 8 * k].reshape(128, 256) for k in range(4)], axis=1
    ).astype(F32)
    gain_all = attn_all[:, 96:104].reshape(128, 256).astype(F32)

    gate_up_mine = jnp.stack(gate_up_parts)
    down_mine = jnp.stack(down_parts)
    gate_all, up_all, down_all = spread_slices(
        jnp.concatenate(
            [jnp.array([0, 2, 3, 1], jnp.int32)[(jnp.arange(4) - xpos) % 4], core[None]]
        ),
        gate_up_mine,
        send(gate_up_mine, CORE_SWAP),
        down_mine,
        send(down_mine, CORE_SWAP),
    )
    return (
        outputs,
        input_grad,
        by_head(0, 128),
        by_head(128, 192),
        by_head(192, 256),
        out_all,
        gate_all,
        up_all,
        down_all,
        gain_all[:, 0],
        gain_all[:, 1],
        gain_all[:8, 2],
        gain_all[:8, 3],
    )


def solution(mesh):
    shard = P("grp", None)
    return jax.shard_map(
        per_device,
        mesh=mesh,
        in_specs=(P("rep", "grp", None), P("rep", None))
        + (shard,) * 7
        + (P("grp"),) * 4
        + (P("rep", "grp", None),),
        out_specs=(P("rep", "grp", None),) * 2 + (shard,) * 7 + (P("grp"),) * 4,
        check_vma=False,
    )
```

profile of v0, /device:TPU:1, one launch (start us, length us, event | category | flops | bytes accessed | tf_op | source)
XLA Modules:
  0.0 417.8 jit_solution(12835460582201858693)
XLA Ops:
  18.1 7.8 %all-to-all-start = ((bf16[8,144,256]{2,1,0:T(8,128)(2,1)}), bf16[8,144,256]{2,1,0:T(8,128)(2,1)S(1)}, u32[]{:S(2)}, u32[]{:S(2)}) async-start(bf16[8,144,256]{2,1,0:T(8,128)(2,1)} %copy.125), calls=%async_computation | async-start | bytes 1179648 | tf_op jit(solution)/shard_map/all_to_all | solution.py:51
  32.8 5.9 %all-to-all-done = bf16[8,144,256]{2,1,0:T(8,128)(2,1)S(1)} async-done(((bf16[8,144,256]{2,1,0:T(8,128)(2,1)}), bf16[8,144,256]{2,1,0:T(8,128)(2,1)S(1)}, u32[]{:S(2)}, u32[]{:S(2)}) %all-to-all-start) | async-done | bytes 589856 | tf_op jit(solution)/shard_map/all_to_all | solution.py:51
  39.8 4.4 %all-to-all-start.1 = ((bf16[8,64,1024]{2,1,0:T(8,128)(2,1)}), bf16[8,64,1024]{2,1,0:T(8,128)(2,1)S(1)}, u32[]{:S(2)}, u32[]{:S(2)}) async-start(bf16[8,64,1024]{2,1,0:T(8,128)(2,1)} %broadcast_in_dim.208), calls=%async_computation.1 | async-start | bytes 2097152 | tf_op jit(solution)/shard_map/all_to_all | solution.py:51
  48.6 11.6 %all-to-all-done.1 = bf16[8,64,1024]{2,1,0:T(8,128)(2,1)S(1)} async-done(((bf16[8,64,1024]{2,1,0:T(8,128)(2,1)}), bf16[8,64,1024]{2,1,0:T(8,128)(2,1)S(1)}, u32[]{:S(2)}, u32[]{:S(2)}) %all-to-all-start.1) | async-done | bytes 1048608 | tf_op jit(solution)/shard_map/all_to_all | solution.py:51
  64.6 7.6 %collective-permute-start = (bf16[8,64,1024]{2,1,0:T(8,128)(2,1)S(1)}, bf16[8,64,1024]{2,1,0:T(8,128)(2,1)}, u32[]{:S(2)}, u32[]{:S(2)}) collective-permute-start(bf16[8,64,1024]{2,1,0:T(8,128)(2,1)S(1)} %all-to-all-done.1), channel_id=1, source_target_pairs={{0,8},{1,9},{2,10},{3,11},{4,12},{5,13},{6,14},{7,15},{8,0},{9,1},... | collective-permute-start | bytes 3145736 | tf_op jit(solution)/shard_map/ppermute | solution.py:47
  82.2 4.5 %all-to-all-start.2 = ((bf16[8,72,1024]{2,1,0:T(8,128)(2,1)}), bf16[8,72,1024]{2,1,0:T(8,128)(2,1)}, u32[]{:S(2)}, u32[]{:S(2)}) async-start(bf16[8,72,1024]{2,1,0:T(8,128)(2,1)} %broadcast_in_dim.219), calls=%async_computation.2 | async-start | bytes 2359296 | tf_op jit(solution)/shard_map/all_to_all | solution.py:51
  91.9 8.4 %attend_forward.1 = (bf16[1536,128]{1,0:T(8,128)(2,1)S(1)}, bf16[1536,1024]{1,0:T(8,128)(2,1)}, bf16[256,1536]{1,0:T(8,128)(2,1)S(1)}, bf16[1536,256]{1,0:T(8,12...) custom-call(s32[16]{0:T(128)S(1)} %bitcast.210, ...), custom_call_target="tpu_custom_call" | custom-call | flops 6000000000 | bytes 14000000 | tf_op jit(solution)/shard_map/attend_forward/pallas_call | solution.py:176
  102.7 14.5 %all_to_all.70 = bf16[8,192,128]{2,1,0:T(8,128)(2,1)} all-to-all(bf16[8,192,128]{2,1,0:T(8,128)(2,1)S(1)} %bitcast.208), channel_id=1, replica_groups=mesh['rep'=16,'grp'=8] {'grp'}, dimensions={0} | all-to-all | bytes 786432 | tf_op jit(solution)/shard_map/all_to_all | solution.py:51
  117.2 4.5 %all-to-all-start.4 = ((bf16[8,64,2304]{2,1,0:T(8,128)(2,1)}), bf16[8,64,2304]{2,1,0:T(8,128)(2,1)}, u32[]{:S(2)}, u32[]{:S(2)}) async-start(bf16[8,64,2304]{2,1,0:T(8,128)(2,1)} %broadcast_in_dim.217), calls=%async_computation.4 | async-start | bytes 4718592 | tf_op jit(solution)/shard_map/all_to_all | solution.py:51
  127.9 6.6 %collective-permute-done.6 = bf16[192,1024]{1,0:T(8,128)(2,1)S(1)} collective-permute-done((bf16[192,1024]{1,0:T(8,128)(2,1)S(1)}, bf16[192,1024]{1,0:T(8,128)(2,1)S(1)}, u32[]{:S(2)}, u32[]{:S(2)}) %collective-permute-start.6) | collective-permute-done | bytes 393248 | tf_op jit(solution)/shard_map/ppermute | solution.py:47
  142.1 8.6 %all-to-all-done.4 = bf16[8,64,2304]{2,1,0:T(8,128)(2,1)} async-done(((bf16[8,64,2304]{2,1,0:T(8,128)(2,1)}), bf16[8,64,2304]{2,1,0:T(8,128)(2,1)}, u32[]{:S(2)}, u32[]{:S(2)}) %all-to-all-start.4) | async-done | bytes 2359328 | tf_op jit(solution)/shard_map/all_to_all | solution.py:51
  152.0 6.0 %collective-permute-done.5 = bf16[8,72,1024]{2,1,0:T(8,128)(2,1)} collective-permute-done((bf16[8,72,1024]{2,1,0:T(8,128)(2,1)}, bf16[8,72,1024]{2,1,0:T(8,128)(2,1)}, u32[]{:S(2)}, u32[]{:S(2)}) %collective-permute-start.5) | collective-permute-done | bytes 1179680 | tf_op jit(solution)/shard_map/ppermute | solution.py:47
  161.3 5.0 %all-to-all-start.5 = ((bf16[8,64,2048]{2,1,0:T(8,128)(2,1)}), bf16[8,64,2048]{2,1,0:T(8,128)(2,1)}, u32[]{:S(2)}, u32[]{:S(2)}) async-start(bf16[8,64,2048]{2,1,0:T(8,128)(2,1)} %broadcast_in_dim.220), calls=%async_computation.5 | async-start | bytes 4194304 | tf_op jit(solution)/shard_map/all_to_all | solution.py:51
  171.3 5.4 %fusion.39 = f32[768,2304]{1,0:T(8,128)S(1)} fusion(bf16[768,1024]{1,0:T(8,128)(2,1)} %constant_dynamic-update-slice_fusion.5, bf16[1024,2304]{1,0:T(8,128)(2,1)S(1)} %bitcast_select_fusion), kind=kOutput, calls=%fused_computation.161 | convolution fusion | flops 3623878656 | bytes 13369344 | tf_op jit(solution)/shard_map/dot_general | solution.py:102
  176.7 5.0 %fusion.3 = (bf16[768,1152]{1,0:T(8,128)(2,1)}, bf16[768,1152]{1,0:T(8,128)(2,1)}, bf16[768,1152]{1,0:T(8,128)(2,1)S(1)}) fusion(f32[768,2304]{1,0:T(8,128)S(1)} %fusion.39, bf16[768,1024]{1,0:T(8,128)(2,1)S(1)} %copy-done.34, bf16[1152,1024]{1,0:T(8,128)(2,1)S(1)} %copy-done.25), kind=kOutput, calls=%fused_computation.10 | convolution fusion | flops 1826095104 | bytes 16318464 | tf_op jit(solution)/shard_map/td,fd->tf/dot_general | solution.py:438
  187.0 4.3 %pad_maximum_fusion = bf16[768,2304]{1,0:T(8,128)(2,1)} fusion(bf16[768,1152]{1,0:T(8,128)(2,1)} %get-tuple-element.142, bf16[768,1152]{1,0:T(8,128)(2,1)} %get-tuple-element.141), kind=kLoop, calls=%fused_computation.11 | loop fusion | flops 7077888 | bytes 7077888 | tf_op jit(solution)/shard_map/concatenate | solution.py:440
  194.1 6.4 %convolution_convert_fusion = bf16[1024,2304]{1,0:T(8,128)(2,1)S(1)} fusion(bf16[768,1024]{1,0:T(8,128)(2,1)} %constant_dynamic-update-slice_fusion.5, bf16[768,2304]{1,0:T(8,128)(2,1)} %pad_maximum_fusion), kind=kOutput, calls=%fused_computation.1 | convolution fusion | flops 3626237952 | bytes 9830400 | tf_op jit(solution)/shard_map/td,tf->df/dot_general | solution.py:443
  203.5 7.0 %all-to-all-start.6 = ((bf16[8,72,1024]{2,1,0:T(8,128)(2,1)}), bf16[8,72,1024]{2,1,0:T(8,128)(2,1)}, u32[]{:S(2)}, u32[]{:S(2)}) async-start(bf16[8,72,1024]{2,1,0:T(8,128)(2,1)} %fusion.5), calls=%async_computation.6 | async-start | bytes 2359296 | tf_op jit(solution)/shard_map/all_to_all | solution.py:51
  210.5 9.0 %fusion.40 = f32[768,1024]{1,0:T(8,128)} fusion(bf16[768,2304]{1,0:T(8,128)(2,1)} %pad_maximum_fusion, bf16[1024,2304]{1,0:T(8,128)(2,1)} %copy-done.16), kind=kOutput, calls=%fused_computation.162 | convolution fusion | flops 3623878656 | bytes 11403264 | tf_op jit(solution)/shard_map/tf,df->td/dot_general | solution.py:445
  226.4 5.7 %all-to-all-start.7 = ((bf16[8,64,2304]{2,1,0:T(8,128)(2,1)}), bf16[8,64,2304]{2,1,0:T(8,128)(2,1)}, u32[]{:S(2)}, u32[]{:S(2)}) async-start(bf16[8,64,2304]{2,1,0:T(8,128)(2,1)} %fusion), calls=%async_computation.7 | async-start | bytes 4718592 | tf_op jit(solution)/shard_map/all_to_all | solution.py:51
  247.5 5.3 %fusion.41 = f32[768,1024]{1,0:T(8,128)} fusion(bf16[768,1152]{1,0:T(8,128)(2,1)} %copy-done.39, bf16[1152,1024]{1,0:T(8,128)(2,1)S(1)} %copy-done.26), kind=kOutput, calls=%fused_computation.163 | convolution fusion | flops 1811939328 | bytes 7274496 | tf_op jit(solution)/shard_map/dot_general | solution.py:102
  276.2 4.6 %broadcast_select_fusion = bf16[8,2,64,2048]{3,2,1,0:T(8,128)(2,1)} fusion(pred[2]{0:T(512)(128)(4,1)S(1)} %iota_compare_fusion, bf16[8,64,2048]{2,1,0:T(8,128)(2,1)} %collective-permute-done.24, bf16[8,64,2048]{2,1,0:T(8,128)(2,1)} %all-to-all-done.5), kind=kLoop, calls=%fused_computation.6 | loop fusion | flops 2097152 | bytes 8388610 | tf_op jit(solution)/shard_map/jit(_where)/select_n | solution.py:349
  280.8 6.4 %all-to-all-start.8 = ((bf16[8,192,128]{2,1,0:T(8,128)(2,1)}), bf16[8,192,128]{2,1,0:T(8,128)(2,1)S(1)}, u32[]{:S(2)}, u32[]{:S(2)}) async-start(bf16[8,192,128]{2,1,0:T(8,128)(2,1)} %bitcast.225), calls=%async_computation.8 | async-start | bytes 786432 | tf_op jit(solution)/shard_map/all_to_all | solution.py:51
  300.8 5.0 %all-to-all-start.9 = ((bf16[8,64,1024]{2,1,0:T(8,128)(2,1)}), bf16[8,64,1024]{2,1,0:T(8,128)(2,1)}, u32[]{:S(2)}, u32[]{:S(2)}) async-start(bf16[8,64,1024]{2,1,0:T(8,128)(2,1)} %fusion.6), calls=%async_computation.9 | async-start | bytes 2097152 | tf_op jit(solution)/shard_map/all_to_all | solution.py:51
  308.1 12.4 %attend_backward.1 = (bf16[1536,256]{1,0:T(8,128)(2,1)}, f32[64,256]{1,0:T(8,128)S(1)}) custom-call(s32[16]{0:T(128)S(1)} %bitcast.211, bf16[256,1536]{1,0:T(8,128)(2,1)S(1)} %get-tuple-element.79.cols_ref, bf16[1536,256]{1,0:T(8,128)(2,1)S(1)} %copy-done.4, bf16[1536,128]{1,0:T(8,128)(2,1)S(1)} %bitcast.207, f32[128,1536]{1,0:T(8,128)S(1)} %copy-done.6, ...), custom_call_target="tpu_custom_call" | custom-call | flops 10000000000 | bytes 8000000 | tf_op jit(solution)/shard_map/attend_backward/pallas_call | solution.py:267
  322.7 6.8 %all-to-all-start.10 = ((bf16[8,192,256]{2,1,0:T(8,128)(2,1)}), bf16[8,192,256]{2,1,0:T(8,128)(2,1)S(1)}, u32[]{:S(2)}, u32[]{:S(2)}) async-start(bf16[8,192,256]{2,1,0:T(8,128)(2,1)} %bitcast.41), calls=%async_computation.10 | async-start | bytes 1572864 | tf_op jit(solution)/shard_map/all_to_all | solution.py:51
  339.4 6.5 %all-to-all-start.11 = ((bf16[8,144,256]{2,1,0:T(8,128)(2,1)}), bf16[8,144,256]{2,1,0:T(8,128)(2,1)S(1)}, u32[]{:S(2)}, u32[]{:S(2)}) async-start(bf16[8,144,256]{2,1,0:T(8,128)(2,1)} %maximum_maximum_fusion), calls=%async_computation.11 | async-start | bytes 1179648 | tf_op jit(solution)/shard_map/all_to_all | solution.py:51
  359.1 10.5 %all-to-all-start.12 = ((bf16[16,104,256]{2,1,0:T(8,128)(2,1)}), bf16[16,104,256]{2,1,0:T(8,128)(2,1)S(1)}, u32[]{:S(2)}, u32[]{:S(2)}) async-start(bf16[16,104,256]{2,1,0:T(8,128)(2,1)} %fusion.25), calls=%async_computation.12 | async-start | bytes 1703936 | tf_op jit(solution)/shard_map/all_to_all | solution.py:536
  377.9 5.1 %all-to-all-done.12 = bf16[16,104,256]{2,1,0:T(8,128)(2,1)S(1)} async-done(((bf16[16,104,256]{2,1,0:T(8,128)(2,1)}), bf16[16,104,256]{2,1,0:T(8,128)(2,1)S(1)}, u32[]{:S(2)}, u32[]{:S(2)}) %all-to-all-start.12) | async-done | bytes 852000 | tf_op jit(solution)/shard_map/all_to_all | solution.py:536
  384.1 5.6 %all-to-all-start.13 = ((bf16[16,104,256]{2,1,0:T(8,128)(2,1)}), bf16[16,104,256]{2,1,0:T(8,128)(2,1)}, u32[]{:S(2)}, u32[]{:S(2)}) async-start(bf16[16,104,256]{2,1,0:T(8,128)(2,1)} %broadcast_in_dim.247), calls=%async_computation.13 | async-start | bytes 1703936 | tf_op jit(solution)/shard_map/all_to_all | solution.py:537
  389.7 4.3 %fusion.11 = (f32[192]{0:T(256)S(1)}, f32[192]{0:T(256)S(1)}, f32[192,1024]{1,0:T(8,128)S(1)}) fusion(bf16[1,192,1024]{2,1,0:T(8,128)(2,1)} %param.15, f32[1024]{0:T(1024)S(1)} %copy-done.36, bf16[192,2048]{1,0:T(8,128)(2,1)} %bitcast.231, bf16[1024,2048]{1,0:T(8,128)(2,1)} %bitcast.216), kind=kOutput, calls=%fused_computation.41 | convolution fusion | flops 806485632 | bytes 6166016 | tf_op jit(solution)/shard_map/tf,df->td/dot_general | solution.py:511
  398.4 4.5 %spread_slices.1 = (f32[128,4608]{1,0:T(8,128)}, f32[128,4608]{1,0:T(8,128)}, f32[576,1024]{1,0:T(8,128)}) custom-call(s32[5]{0:T(128)S(1)} %pad_add_fusion.index_ref, bf16[4,64,2304]{2,1,0:T(8,128)(2,1)S(1)} %pad_maximum_fusion.1.mine_ref, bf16[4,64,2304]{2,1,0:T(8,128)(2,1)S(1)} %collective-permute-done.33.other_ref, ...), custom_call_target="tpu_custom_call" | custom-call | flops 10000000 | bytes 10000000 | tf_op jit(solution)/shard_map/spread_slices/pallas_call | solution.py:313
  (307 shorter events, 187.4 us)
Async XLA Ops:
  7.2 84.7 %all-gather.3.cloned.1.call-start = ((), (), s32[]{:S(2)}) async-start(), calls=%async_computation.14 | async-start | bytes 3538944 | tf_op jit(solution)/shard_map/all_gather | solution.py:372
  7.9 65.2 %collective-permute-start.1 = (bf16[192,1024]{1,0:T(8,128)(2,1)}, bf16[192,1024]{1,0:T(8,128)(2,1)}, u32[]{:S(2)}, u32[]{:S(2)}) collective-permute-start(bf16[192,1024]{1,0:T(8,128)(2,1)} %bitcast.217), channel_id=1, source_target_pairs={{0,32},{1,33},{2,34},{3,35},{4,36},{5,37},{6,38},{7,39},{8,40},{9,... | collective-permute-start | bytes 1179656 | tf_op jit(solution)/shard_map/ppermute | solution.py:47
  10.0 64.1 %collective-permute-start.2 = (bf16[192,1024]{1,0:T(8,128)(2,1)}, bf16[192,1024]{1,0:T(8,128)(2,1)}, u32[]{:S(2)}, u32[]{:S(2)}) collective-permute-start(bf16[192,1024]{1,0:T(8,128)(2,1)} %bitcast.218), channel_id=1, source_target_pairs={{0,96},{1,97},{2,98},{3,99},{4,100},{5,101},{6,102},{7,103},{8,104... | collective-permute-start | bytes 1179656 | tf_op jit(solution)/shard_map/ppermute | solution.py:47
  18.1 20.7 %all-to-all-start = ((bf16[8,144,256]{2,1,0:T(8,128)(2,1)}), bf16[8,144,256]{2,1,0:T(8,128)(2,1)S(1)}, u32[]{:S(2)}, u32[]{:S(2)}) async-start(bf16[8,144,256]{2,1,0:T(8,128)(2,1)} %copy.125), calls=%async_computation | async-start | bytes 1179648 | tf_op jit(solution)/shard_map/all_to_all | solution.py:51
  39.8 20.4 %all-to-all-start.1 = ((bf16[8,64,1024]{2,1,0:T(8,128)(2,1)}), bf16[8,64,1024]{2,1,0:T(8,128)(2,1)S(1)}, u32[]{:S(2)}, u32[]{:S(2)}) async-start(bf16[8,64,1024]{2,1,0:T(8,128)(2,1)} %broadcast_in_dim.208), calls=%async_computation.1 | async-start | bytes 2097152 | tf_op jit(solution)/shard_map/all_to_all | solution.py:51
  64.6 24.5 %collective-permute-start = (bf16[8,64,1024]{2,1,0:T(8,128)(2,1)S(1)}, bf16[8,64,1024]{2,1,0:T(8,128)(2,1)}, u32[]{:S(2)}, u32[]{:S(2)}) collective-permute-start(bf16[8,64,1024]{2,1,0:T(8,128)(2,1)S(1)} %all-to-all-done.1), channel_id=1, source_target_pairs={{0,8},{1,9},{2,10},{3,11},{4,12},{5,13},{6,14},{7,15},{8,0},{9,1},... | collective-permute-start | bytes 3145736 | tf_op jit(solution)/shard_map/ppermute | solution.py:47
  74.1 13.6 %collective-permute-start.3 = (bf16[96,1024]{1,0:T(8,128)(2,1)S(1)}, bf16[96,1024]{1,0:T(8,128)(2,1)S(1)}, u32[]{:S(2)}, u32[]{:S(2)}) collective-permute-start(bf16[96,1024]{1,0:T(8,128)(2,1)S(1)} %slice.247), channel_id=1, source_target_pairs={{0,32},{1,33},{2,34},{3,35},{4,36},{5,37},{6,38},{7,39},{8,40},{9,... | collective-permute-start | bytes 589832 | tf_op jit(solution)/shard_map/ppermute | solution.py:47
  82.2 20.5 %all-to-all-start.2 = ((bf16[8,72,1024]{2,1,0:T(8,128)(2,1)}), bf16[8,72,1024]{2,1,0:T(8,128)(2,1)}, u32[]{:S(2)}, u32[]{:S(2)}) async-start(bf16[8,72,1024]{2,1,0:T(8,128)(2,1)} %broadcast_in_dim.219), calls=%async_computation.2 | async-start | bytes 2359296 | tf_op jit(solution)/shard_map/all_to_all | solution.py:51
  117.2 33.5 %all-to-all-start.4 = ((bf16[8,64,2304]{2,1,0:T(8,128)(2,1)}), bf16[8,64,2304]{2,1,0:T(8,128)(2,1)}, u32[]{:S(2)}, u32[]{:S(2)}) async-start(bf16[8,64,2304]{2,1,0:T(8,128)(2,1)} %broadcast_in_dim.217), calls=%async_computation.4 | async-start | bytes 4718592 | tf_op jit(solution)/shard_map/all_to_all | solution.py:51
  150.6 15.7 %collective-permute-start.10 = (bf16[8,64,2304]{2,1,0:T(8,128)(2,1)}, bf16[8,64,2304]{2,1,0:T(8,128)(2,1)}, u32[]{:S(2)}, u32[]{:S(2)}) collective-permute-start(bf16[8,64,2304]{2,1,0:T(8,128)(2,1)} %all-to-all-done.4), channel_id=1, source_target_pairs={{0,8},{1,9},{2,10},{3,11},{4,12},{5,13},{6,14},{7,15},{8,0},{9,1},... | collective-permute-start | bytes 7077896 | tf_op jit(solution)/shard_map/ppermute | solution.py:47
  161.3 32.8 %all-to-all-start.5 = ((bf16[8,64,2048]{2,1,0:T(8,128)(2,1)}), bf16[8,64,2048]{2,1,0:T(8,128)(2,1)}, u32[]{:S(2)}, u32[]{:S(2)}) async-start(bf16[8,64,2048]{2,1,0:T(8,128)(2,1)} %broadcast_in_dim.220), calls=%async_computation.5 | async-start | bytes 4194304 | tf_op jit(solution)/shard_map/all_to_all | solution.py:51
  203.3 16.2 %collective-permute-start.12 = (bf16[8,64,2304]{2,1,0:T(8,128)(2,1)}, bf16[8,64,2304]{2,1,0:T(8,128)(2,1)}, u32[]{:S(2)}, u32[]{:S(2)}) collective-permute-start(bf16[8,64,2304]{2,1,0:T(8,128)(2,1)} %dynamic-slice_bitcast_fusion), channel_id=1, source_target_pairs={{0,8},{1,9},{2,10},{3,11},{4,12},{5,13},{6,14},{7,15},{8,0},{9,1},... | collective-permute-start | bytes 7077896 | tf_op jit(solution)/shard_map/ppermute | solution.py:47
  203.5 22.9 %all-to-all-start.6 = ((bf16[8,72,1024]{2,1,0:T(8,128)(2,1)}), bf16[8,72,1024]{2,1,0:T(8,128)(2,1)}, u32[]{:S(2)}, u32[]{:S(2)}) async-start(bf16[8,72,1024]{2,1,0:T(8,128)(2,1)} %fusion.5), calls=%async_computation.6 | async-start | bytes 2359296 | tf_op jit(solution)/shard_map/all_to_all | solution.py:51
  226.4 34.8 %all-to-all-start.7 = ((bf16[8,64,2304]{2,1,0:T(8,128)(2,1)}), bf16[8,64,2304]{2,1,0:T(8,128)(2,1)}, u32[]{:S(2)}, u32[]{:S(2)}) async-start(bf16[8,64,2304]{2,1,0:T(8,128)(2,1)} %fusion), calls=%async_computation.7 | async-start | bytes 4718592 | tf_op jit(solution)/shard_map/all_to_all | solution.py:51
  239.8 36.4 %collective-permute-start.24 = (bf16[8,64,2048]{2,1,0:T(8,128)(2,1)}, bf16[8,64,2048]{2,1,0:T(8,128)(2,1)}, u32[]{:S(2)}, u32[]{:S(2)}) collective-permute-start(bf16[8,64,2048]{2,1,0:T(8,128)(2,1)} %all-to-all-done.5), channel_id=1, source_target_pairs={{0,8},{1,9},{2,10},{3,11},{4,12},{5,13},{6,14},{7,15},{8,0},{9,1},... | collective-permute-start | bytes 6291464 | tf_op jit(solution)/shard_map/ppermute | solution.py:47
  269.2 21.4 %collective-permute-start.17 = (bf16[8,64,1024]{2,1,0:T(8,128)(2,1)}, bf16[8,64,1024]{2,1,0:T(8,128)(2,1)}, u32[]{:S(2)}, u32[]{:S(2)}) collective-permute-start(bf16[8,64,1024]{2,1,0:T(8,128)(2,1)} %dynamic-slice_bitcast_fusion.2), channel_id=1, source_target_pairs={{0,8},{1,9},{2,10},{3,11},{4,12},{5,13},{6,14},{7,15},{8,0},{9,1},... | collective-permute-start | bytes 3145736 | tf_op jit(solution)/shard_map/ppermute | solution.py:47
  273.2 15.6 %collective-permute-start.18 = (bf16[64,2304]{1,0:T(8,128)(2,1)}, bf16[64,2304]{1,0:T(8,128)(2,1)}, u32[]{:S(2)}, u32[]{:S(2)}) collective-permute-start(bf16[64,2304]{1,0:T(8,128)(2,1)} %reduce_sum.131), channel_id=1, source_target_pairs={{0,16},{1,17},{2,18},{3,19},{4,20},{5,21},{6,22},{7,23},{8,24},{9,... | collective-permute-start | bytes 884744 | tf_op jit(solution)/shard_map/ppermute | solution.py:47
  280.8 14.5 %all-to-all-start.8 = ((bf16[8,192,128]{2,1,0:T(8,128)(2,1)}), bf16[8,192,128]{2,1,0:T(8,128)(2,1)S(1)}, u32[]{:S(2)}, u32[]{:S(2)}) async-start(bf16[8,192,128]{2,1,0:T(8,128)(2,1)} %bitcast.225), calls=%async_computation.8 | async-start | bytes 786432 | tf_op jit(solution)/shard_map/all_to_all | solution.py:51
  295.2 41.1 %collective-permute-start.25 = (bf16[64,2304]{1,0:T(8,128)(2,1)}, bf16[64,2304]{1,0:T(8,128)(2,1)}, u32[]{:S(2)}, u32[]{:S(2)}) collective-permute-start(bf16[64,2304]{1,0:T(8,128)(2,1)} %add_convert_fusion.1), channel_id=1, source_target_pairs={{0,32},{1,33},{2,34},{3,35},{4,36},{5,37},{6,38},{7,39},{8,40},{9,... | collective-permute-start | bytes 884744 | tf_op jit(solution)/shard_map/ppermute | solution.py:47
  295.2 38.8 %collective-permute-start.26 = (bf16[64,2304]{1,0:T(8,128)(2,1)}, bf16[64,2304]{1,0:T(8,128)(2,1)}, u32[]{:S(2)}, u32[]{:S(2)}) collective-permute-start(bf16[64,2304]{1,0:T(8,128)(2,1)} %add_convert_fusion.1), channel_id=1, source_target_pairs={{0,96},{1,97},{2,98},{3,99},{4,100},{5,101},{6,102},{7,103},{8,104... | collective-permute-start | bytes 884744 | tf_op jit(solution)/shard_map/ppermute | solution.py:47
  298.1 33.4 %collective-permute-start.29 = (bf16[72,1024]{1,0:T(8,128)(2,1)}, bf16[72,1024]{1,0:T(8,128)(2,1)}, u32[]{:S(2)}, u32[]{:S(2)}) collective-permute-start(bf16[72,1024]{1,0:T(8,128)(2,1)} %add_convert_fusion.6), channel_id=1, source_target_pairs={{0,32},{1,33},{2,34},{3,35},{4,36},{5,37},{6,38},{7,39},{8,40},{9,... | collective-permute-start | bytes 442376 | tf_op jit(solution)/shard_map/ppermute | solution.py:47
  298.1 32.4 %collective-permute-start.30 = (bf16[72,1024]{1,0:T(8,128)(2,1)}, bf16[72,1024]{1,0:T(8,128)(2,1)}, u32[]{:S(2)}, u32[]{:S(2)}) collective-permute-start(bf16[72,1024]{1,0:T(8,128)(2,1)} %add_convert_fusion.6), channel_id=1, source_target_pairs={{0,96},{1,97},{2,98},{3,99},{4,100},{5,101},{6,102},{7,103},{8,104... | collective-permute-start | bytes 442376 | tf_op jit(solution)/shard_map/ppermute | solution.py:47
  300.8 21.9 %all-to-all-start.9 = ((bf16[8,64,1024]{2,1,0:T(8,128)(2,1)}), bf16[8,64,1024]{2,1,0:T(8,128)(2,1)}, u32[]{:S(2)}, u32[]{:S(2)}) async-start(bf16[8,64,1024]{2,1,0:T(8,128)(2,1)} %fusion.6), calls=%async_computation.9 | async-start | bytes 2097152 | tf_op jit(solution)/shard_map/all_to_all | solution.py:51
  322.7 16.7 %all-to-all-start.10 = ((bf16[8,192,256]{2,1,0:T(8,128)(2,1)}), bf16[8,192,256]{2,1,0:T(8,128)(2,1)S(1)}, u32[]{:S(2)}, u32[]{:S(2)}) async-start(bf16[8,192,256]{2,1,0:T(8,128)(2,1)} %bitcast.41), calls=%async_computation.10 | async-start | bytes 1572864 | tf_op jit(solution)/shard_map/all_to_all | solution.py:51
  339.4 15.4 %all-to-all-start.11 = ((bf16[8,144,256]{2,1,0:T(8,128)(2,1)}), bf16[8,144,256]{2,1,0:T(8,128)(2,1)S(1)}, u32[]{:S(2)}, u32[]{:S(2)}) async-start(bf16[8,144,256]{2,1,0:T(8,128)(2,1)} %maximum_maximum_fusion), calls=%async_computation.11 | async-start | bytes 1179648 | tf_op jit(solution)/shard_map/all_to_all | solution.py:51
  348.8 20.8 %collective-permute-start.20 = (bf16[96,1024]{1,0:T(8,128)(2,1)S(1)}, bf16[96,1024]{1,0:T(8,128)(2,1)S(1)}, u32[]{:S(2)}, u32[]{:S(2)}) collective-permute-start(bf16[96,1024]{1,0:T(8,128)(2,1)S(1)} %get-tuple-element.148), channel_id=1, source_target_pairs={{0,32},{1,33},{2,34},{3,35},{4,36},{5,37},{6,38},{7,39},{8,40},{9,... | collective-permute-start | bytes 589832 | tf_op jit(solution)/shard_map/ppermute | solution.py:47
  348.8 20.8 %collective-permute-start.22 = (bf16[96,1024]{1,0:T(8,128)(2,1)S(1)}, bf16[96,1024]{1,0:T(8,128)(2,1)S(1)}, u32[]{:S(2)}, u32[]{:S(2)}) collective-permute-start(bf16[96,1024]{1,0:T(8,128)(2,1)S(1)} %get-tuple-element.149), channel_id=1, source_target_pairs={{0,96},{1,97},{2,98},{3,99},{4,100},{5,101},{6,102},{7,103},{8,104... | collective-permute-start | bytes 589832 | tf_op jit(solution)/shard_map/ppermute | solution.py:47
  359.1 23.9 %all-to-all-start.12 = ((bf16[16,104,256]{2,1,0:T(8,128)(2,1)}), bf16[16,104,256]{2,1,0:T(8,128)(2,1)S(1)}, u32[]{:S(2)}, u32[]{:S(2)}) async-start(bf16[16,104,256]{2,1,0:T(8,128)(2,1)} %fusion.25), calls=%async_computation.12 | async-start | bytes 1703936 | tf_op jit(solution)/shard_map/all_to_all | solution.py:536
  371.6 23.9 %collective-permute-start.23 = (bf16[192,1024]{1,0:T(8,128)(2,1)}, bf16[192,1024]{1,0:T(8,128)(2,1)}, u32[]{:S(2)}, u32[]{:S(2)}) collective-permute-start(bf16[192,1024]{1,0:T(8,128)(2,1)} %pad_maximum_fusion.8), channel_id=1, source_target_pairs={{0,96},{1,97},{2,98},{3,99},{4,100},{5,101},{6,102},{7,103},{8,104... | collective-permute-start | bytes 1179656 | tf_op jit(solution)/shard_map/ppermute | solution.py:47
  375.4 23.0 %collective-permute-start.33 = (bf16[4,64,2304]{2,1,0:T(8,128)(2,1)S(1)}, bf16[4,64,2304]{2,1,0:T(8,128)(2,1)S(1)}, u32[]{:S(2)}, u32[]{:S(2)}) collective-permute-start(bf16[4,64,2304]{2,1,0:T(8,128)(2,1)S(1)} %pad_maximum_fusion.1.mine_ref), channel_id=1, source_target_pairs={{0,8},{1,9},{2,10},{3,11},{4,12},{5,13},{6,14},{7,15},{8,0},{9,1},... | collective-permute-start | bytes 3538952 | tf_op jit(solution)/shard_map/ppermute | solution.py:47
  376.9 18.6 %collective-permute-start.21 = (bf16[192,1024]{1,0:T(8,128)(2,1)}, bf16[192,1024]{1,0:T(8,128)(2,1)}, u32[]{:S(2)}, u32[]{:S(2)}) collective-permute-start(bf16[192,1024]{1,0:T(8,128)(2,1)} %pad_maximum_fusion.7), channel_id=1, source_target_pairs={{0,32},{1,33},{2,34},{3,35},{4,36},{5,37},{6,38},{7,39},{8,40},{9,... | collective-permute-start | bytes 1179656 | tf_op jit(solution)/shard_map/ppermute | solution.py:47
  384.1 19.2 %all-to-all-start.13 = ((bf16[16,104,256]{2,1,0:T(8,128)(2,1)}), bf16[16,104,256]{2,1,0:T(8,128)(2,1)}, u32[]{:S(2)}, u32[]{:S(2)}) async-start(bf16[16,104,256]{2,1,0:T(8,128)(2,1)} %broadcast_in_dim.247), calls=%async_computation.13 | async-start | bytes 1703936 | tf_op jit(solution)/shard_map/all_to_all | solution.py:537
  (57 other events, 409.5 us)
Sparse Core Ops, SparseCore 0:
  10.3 74.6 all-gather.2
where the time goes:
time: 425 us; the launch traced here: 418 us
  starting transfers between devices  125 us (29%)
  other arithmetic  66 us (16%)
  local copies, waits for them, and re-layouts  64.8 us (15%)
  waiting for transfers between devices  62.7 us (15%)
  matrix products  43.8 us (10%)
  Pallas kernels  25.3 us (6%)
  between operations  15.4 us (4%)
  blocking collectives  14.5 us (3%)
    all_to_all x11, starting transfers between devices, exchange_grp(): return lax.all_to_all(value, 'grp', 0, 0)  63.5 us
    ppermute x35, starting transfers between devices, send(): return lax.ppermute(value, AXES, perm)  45.8 us
    all_to_all x11, waiting for transfers between devices, exchange_grp(): return lax.all_to_all(value, 'grp', 0, 0)  35.4 us
    unnamed x98, local copies, waits for them, and re-layouts  29 us
    ppermute x35, waiting for transfers between devices, send(): return lax.ppermute(value, AXES, perm)  21.2 us
    all_to_all x1, blocking collectives, exchange_grp(): return lax.all_to_all(value, 'grp', 0, 0)  14.5 us
    select_n x4, other arithmetic, both_cores(): jnp.where(picked, mine[:, None], other[:, None]).reshape(-1, mine.shape[-1])  13.5 us
    dot_general x3, matrix products, dot(): return jnp.dot(a, b, preferred_element_type=F32)  13.2 us
  transfers between devices with their start and end apart: 49, of which 17 were waited for; matrix products, arithmetic and copies ran while one was open for 36% of the time, Pallas kernels for 6%

commit v1 on v0

--- a/solution.py
+++ b/solution.py
@@ -412,8 +412,9 @@
 
     input_ffn_own = rms_norm(x_mid, ffn_scale).astype(BF16)
     input_ffn = jnp.concatenate(x_gather(input_ffn_own), axis=0)
-    down_full = both_cores(down_half)
-    qkv_sent, gate_up_half, input_ffn = tie(qkv_sent, gate_up_half, input_ffn)
+    qkv_sent, gate_up_half, input_ffn, down_full = tie(
+        qkv_sent, gate_up_half, input_ffn, both_cores(down_half)
+    )
     qkv_half = exchange_grp(qkv_sent)
     gate_up_full = both_cores(gate_up_half)
 
@@ -448,8 +449,9 @@
     grad_input_part, gate_up_sent, down_got = tie(grad_input_part, gate_up_sent, down_got)
     gate_up_got = exchange_grp(gate_up_sent)
     grad_input_ffn = x_reduce(grad_input_part.reshape(4, rows, 1024))
-    grad_input_ffn, gate_up_got = tie(grad_input_ffn, gate_up_got)
-    down_part = dot(hidden, down_full)
+    grad_input_ffn, gate_up_got, down_sum, down_part = tie(
+        grad_input_ffn, gate_up_got, total(down_got), dot(hidden, down_full)
+    )
 
     _, pull_ffn_norm = jax.vjp(rms_norm, x_mid, ffn_scale)
     grad_mid_norm, ffn_gain_grad = pull_ffn_norm(grad_input_ffn)
@@ -458,13 +460,13 @@
     grad_mixed = jnp.einsum(
         "td,fd->tf", grad_attn, out_full, preferred_element_type=F32
     ).astype(BF16)
-    grad_sent, grad_attn, gate_up_got, down_got = tie(
-        grad_mixed.reshape(rows, 8, 128).transpose(1, 0, 2), grad_attn, gate_up_got, down_got
+    grad_sent, grad_attn, gate_up_got = tie(
+        grad_mixed.reshape(rows, 8, 128).transpose(1, 0, 2), grad_attn, gate_up_got
     )
     grad_heads = exchange_grp(grad_sent)
     out_grad = jnp.einsum("tf,td->fd", mixed, grad_attn, preferred_element_type=F32)
     gate_up_sum = y_sum(total(gate_up_got))
-    down_sum = y_sum(total(down_got))
+    down_sum = y_sum(down_sum)
     out_sent = core_sum(out_grad, 64)
     grad_heads, out_sent, gate_up_sum, down_sum = tie(
         grad_heads, out_sent, gate_up_sum, down_sum
@@ -501,7 +503,7 @@
     qkv_sent = jnp.concatenate(
         [qkv_grad.astype(BF16).reshape(8, 128, 256), gain_parts.astype(BF16)], axis=1
     )
-    qkv_sent, packed = tie(qkv_sent, packed)
+    qkv_sent, packed, qkv_half = tie(qkv_sent, packed, qkv_half)
     qkv_got = exchange_grp(qkv_sent)
     qkv_got, gate_up_parts, down_parts = tie(qkv_got, gate_up_parts, down_parts)
     grad_packed = packed.transpose(1, 0, 2)
@@ -533,7 +535,8 @@
         + [gain_columns.reshape(16, 8, 256)],
         axis=1,
     )
-    attn_part = jnp.sum(lax.all_to_all(attn_rows, "rep", 0, 0).astype(F32), axis=0).astype(BF16)
+    rep_got, outputs = tie(lax.all_to_all(attn_rows, "rep", 0, 0), outputs)
+    attn_part = jnp.sum(rep_got.astype(F32), axis=0).astype(BF16)
     attn_all = lax.all_to_all(
         jnp.broadcast_to(attn_part[None], (16, 104, 256)), "rep", 0, 0
     )

time: 425 us -> 421 us (level)
  starting transfers between devices: 125 us -> 131 us
  matrix products: 43.8 us -> 38.1 us
  waiting for transfers between devices: 62.7 us -> 58 us
    ppermute x35, starting transfers between devices: 45.8 us -> 59.9 us  [send(): return lax.ppermute(value, AXES, perm)]
    all_to_all x11, waiting for transfers between devices: 35.4 us -> 26.7 us  [exchange_grp(): return lax.all_to_all(value, 'grp', 0, 0)]
    all_to_all x1, starting transfers between devices: 10.5 us -> 3.64 us  [per_device(): rep_got, outputs = tie(lax.all_to_all(attn_rows, 'rep', 0, 0), outputs)]
    all_to_all x1, waiting for transfers between devices: 0.35 us -> 5.92 us  [per_device(): lax.all_to_all(jnp.broadcast_to(attn_part[None], (16, 104, 256)), 'rep',...]
    unnamed x98 -> x110, local copies, waits for them, and re-layouts: 29 us -> 31 us
  transfers between devices with their start and end apart: 49 -> 49, of which waited for: 17 -> 15; matrix products, arithmetic and copies ran while one was open for 36% -> 34% of each run, Pallas kernels for 6% -> 6%
where the time goes in v1:
time: 421 us; the launch traced here: 413 us
  starting transfers between devices  131 us (31%)
  local copies, waits for them, and re-layouts  65.7 us (16%)
  other arithmetic  65.3 us (16%)
  waiting for transfers between devices  58 us (14%)
  matrix products  38.1 us (9%)
  Pallas kernels  25.3 us (6%)
  between operations  15.5 us (4%)
  blocking collectives  14.4 us (3%)
    all_to_all x11, starting transfers between devices, exchange_grp(): return lax.all_to_all(value, 'grp', 0, 0)  62.5 us
    ppermute x35, starting transfers between devices, send(): return lax.ppermute(value, AXES, perm)  59.9 us
    unnamed x110, local copies, waits for them, and re-layouts  31 us
    all_to_all x11, waiting for transfers between devices, exchange_grp(): return lax.all_to_all(value, 'grp', 0, 0)  26.7 us
    ppermute x35, waiting for transfers between devices, send(): return lax.ppermute(value, AXES, perm)  18.8 us
    all_to_all x1, blocking collectives, exchange_grp(): return lax.all_to_all(value, 'grp', 0, 0)  14.4 us
    pallas_call x1, Pallas kernels, attend_backward(): pl.pallas_call(backward_kernel, out_shape=(jax.ShapeDtypeStruct((SEQ, 256...  12.4 us
    select_n x4, other arithmetic, both_cores(): jnp.where(picked, mine[:, None], other[:, None]).reshape(-1, mine.shape[-1])  11.7 us
  transfers between devices with their start and end apart: 49, of which 15 were waited for; matrix products, arithmetic and copies ran while one was open for 34% of the time, Pallas kernels for 6%

profile of v1, /device:TPU:1, one launch (start us, length us, event | category | flops | bytes accessed | tf_op | source)
XLA Modules:
  0.0 413.5 jit_solution(10848394576341333739)
XLA Ops:
  18.1 7.8 %all-to-all-start = ((bf16[8,144,256]{2,1,0:T(8,128)(2,1)}), bf16[8,144,256]{2,1,0:T(8,128)(2,1)S(1)}, u32[]{:S(2)}, u32[]{:S(2)}) async-start(bf16[8,144,256]{2,1,0:T(8,128)(2,1)} %copy.125), calls=%async_computation | async-start | bytes 1179648 | tf_op jit(solution)/shard_map/all_to_all | solution.py:51
  32.8 5.9 %all-to-all-done = bf16[8,144,256]{2,1,0:T(8,128)(2,1)S(1)} async-done(((bf16[8,144,256]{2,1,0:T(8,128)(2,1)}), bf16[8,144,256]{2,1,0:T(8,128)(2,1)S(1)}, u32[]{:S(2)}, u32[]{:S(2)}) %all-to-all-start) | async-done | bytes 589856 | tf_op jit(solution)/shard_map/all_to_all | solution.py:51
  39.8 4.4 %all-to-all-start.1 = ((bf16[8,64,1024]{2,1,0:T(8,128)(2,1)}), bf16[8,64,1024]{2,1,0:T(8,128)(2,1)S(1)}, u32[]{:S(2)}, u32[]{:S(2)}) async-start(bf16[8,64,1024]{2,1,0:T(8,128)(2,1)} %broadcast_in_dim.208), calls=%async_computation.1 | async-start | bytes 2097152 | tf_op jit(solution)/shard_map/all_to_all | solution.py:51
  48.6 11.6 %all-to-all-done.1 = bf16[8,64,1024]{2,1,0:T(8,128)(2,1)S(1)} async-done(((bf16[8,64,1024]{2,1,0:T(8,128)(2,1)}), bf16[8,64,1024]{2,1,0:T(8,128)(2,1)S(1)}, u32[]{:S(2)}, u32[]{:S(2)}) %all-to-all-start.1) | async-done | bytes 1048608 | tf_op jit(solution)/shard_map/all_to_all | solution.py:51
  64.6 7.6 %collective-permute-start = (bf16[8,64,1024]{2,1,0:T(8,128)(2,1)S(1)}, bf16[8,64,1024]{2,1,0:T(8,128)(2,1)}, u32[]{:S(2)}, u32[]{:S(2)}) collective-permute-start(bf16[8,64,1024]{2,1,0:T(8,128)(2,1)S(1)} %all-to-all-done.1), channel_id=1, source_target_pairs={{0,8},{1,9},{2,10},{3,11},{4,12},{5,13},{6,14},{7,15},{8,0},{9,1},... | collective-permute-start | bytes 3145736 | tf_op jit(solution)/shard_map/ppermute | solution.py:47
  82.2 4.5 %all-to-all-start.2 = ((bf16[8,72,1024]{2,1,0:T(8,128)(2,1)}), bf16[8,72,1024]{2,1,0:T(8,128)(2,1)}, u32[]{:S(2)}, u32[]{:S(2)}) async-start(bf16[8,72,1024]{2,1,0:T(8,128)(2,1)} %broadcast_in_dim.219), calls=%async_computation.2 | async-start | bytes 2359296 | tf_op jit(solution)/shard_map/all_to_all | solution.py:51
  91.9 8.4 %attend_forward.1 = (bf16[1536,128]{1,0:T(8,128)(2,1)S(1)}, bf16[1536,1024]{1,0:T(8,128)(2,1)}, bf16[256,1536]{1,0:T(8,128)(2,1)S(1)}, bf16[1536,256]{1,0:T(8,12...) custom-call(s32[16]{0:T(128)S(1)} %bitcast.210, ...), custom_call_target="tpu_custom_call" | custom-call | flops 6000000000 | bytes 14000000 | tf_op jit(solution)/shard_map/attend_forward/pallas_call | solution.py:176
  102.7 14.4 %all_to_all.70 = bf16[8,192,128]{2,1,0:T(8,128)(2,1)} all-to-all(bf16[8,192,128]{2,1,0:T(8,128)(2,1)S(1)} %bitcast.208), channel_id=1, replica_groups=mesh['rep'=16,'grp'=8] {'grp'}, dimensions={0} | all-to-all | bytes 786432 | tf_op jit(solution)/shard_map/all_to_all | solution.py:51
  117.1 4.5 %all-to-all-start.4 = ((bf16[8,64,2304]{2,1,0:T(8,128)(2,1)}), bf16[8,64,2304]{2,1,0:T(8,128)(2,1)}, u32[]{:S(2)}, u32[]{:S(2)}) async-start(bf16[8,64,2304]{2,1,0:T(8,128)(2,1)} %broadcast_in_dim.217), calls=%async_computation.4 | async-start | bytes 4718592 | tf_op jit(solution)/shard_map/all_to_all | solution.py:51
  131.6 9.4 %collective-permute-done.5 = bf16[192,1024]{1,0:T(8,128)(2,1)S(1)} collective-permute-done((bf16[192,1024]{1,0:T(8,128)(2,1)}, bf16[192,1024]{1,0:T(8,128)(2,1)S(1)}, u32[]{:S(2)}, u32[]{:S(2)}) %collective-permute-start.5) | collective-permute-done | bytes 393248 | tf_op jit(solution)/shard_map/ppermute | solution.py:47
  154.3 7.2 %all-to-all-start.5 = ((bf16[8,64,2048]{2,1,0:T(8,128)(2,1)}), bf16[8,64,2048]{2,1,0:T(8,128)(2,1)}, u32[]{:S(2)}, u32[]{:S(2)}) async-start(bf16[8,64,2048]{2,1,0:T(8,128)(2,1)} %broadcast_in_dim.220), calls=%async_computation.5 | async-start | bytes 4194304 | tf_op jit(solution)/shard_map/all_to_all | solution.py:51
  166.7 3.8 fusion.39
  170.6 5.0 %fusion.3 = (bf16[768,1152]{1,0:T(8,128)(2,1)}, bf16[768,1152]{1,0:T(8,128)(2,1)}, bf16[768,1152]{1,0:T(8,128)(2,1)S(1)}) fusion(f32[768,2304]{1,0:T(8,128)S(1)} %fusion.39, bf16[768,1024]{1,0:T(8,128)(2,1)S(1)} %copy-done.33, bf16[1152,1024]{1,0:T(8,128)(2,1)S(1)} %copy-done.23), kind=kOutput, calls=%fused_computation.10 | convolution fusion | flops 1826095104 | bytes 16318464 | tf_op jit(solution)/shard_map/td,fd->tf/dot_general | solution.py:439
  180.5 4.3 %pad_maximum_fusion = bf16[768,2304]{1,0:T(8,128)(2,1)} fusion(bf16[768,1152]{1,0:T(8,128)(2,1)} %get-tuple-element.152, bf16[768,1152]{1,0:T(8,128)(2,1)} %get-tuple-element.151), kind=kLoop, calls=%fused_computation.11 | loop fusion | flops 7077888 | bytes 7077888 | tf_op jit(solution)/shard_map/concatenate | solution.py:441
  187.9 6.4 %convolution_convert_fusion = bf16[1024,2304]{1,0:T(8,128)(2,1)S(1)} fusion(bf16[768,1024]{1,0:T(8,128)(2,1)} %constant_dynamic-update-slice_fusion.5, bf16[768,2304]{1,0:T(8,128)(2,1)} %pad_maximum_fusion), kind=kOutput, calls=%fused_computation.1 | convolution fusion | flops 3626237952 | bytes 9830400 | tf_op jit(solution)/shard_map/td,tf->df/dot_general | solution.py:444
  198.4 5.5 %all-to-all-start.6 = ((bf16[8,72,1024]{2,1,0:T(8,128)(2,1)}), bf16[8,72,1024]{2,1,0:T(8,128)(2,1)}, u32[]{:S(2)}, u32[]{:S(2)}) async-start(bf16[8,72,1024]{2,1,0:T(8,128)(2,1)} %fusion.5), calls=%async_computation.6 | async-start | bytes 2359296 | tf_op jit(solution)/shard_map/all_to_all | solution.py:51
  203.9 9.0 %fusion.40 = f32[768,1024]{1,0:T(8,128)} fusion(bf16[768,2304]{1,0:T(8,128)(2,1)} %pad_maximum_fusion, bf16[1024,2304]{1,0:T(8,128)(2,1)} %copy-done.16), kind=kOutput, calls=%fused_computation.162 | convolution fusion | flops 3623878656 | bytes 11403264 | tf_op jit(solution)/shard_map/tf,df->td/dot_general | solution.py:446
  213.0 3.7 fusion
  219.8 5.7 %all-to-all-start.7 = ((bf16[8,64,2304]{2,1,0:T(8,128)(2,1)}), bf16[8,64,2304]{2,1,0:T(8,128)(2,1)}, u32[]{:S(2)}, u32[]{:S(2)}) async-start(bf16[8,64,2304]{2,1,0:T(8,128)(2,1)} %fusion), calls=%async_computation.7 | async-start | bytes 4718592 | tf_op jit(solution)/shard_map/all_to_all | solution.py:51
  230.9 4.5 %collective-permute-done.13 = bf16[96,1024]{1,0:T(8,128)(2,1)S(1)} collective-permute-done((bf16[96,1024]{1,0:T(8,128)(2,1)S(1)}, bf16[96,1024]{1,0:T(8,128)(2,1)S(1)}, u32[]{:S(2)}, u32[]{:S(2)}) %collective-permute-start.13) | collective-permute-done | bytes 196640 | tf_op jit(solution)/shard_map/ppermute | solution.py:47
  240.9 3.9 fusion.41
  250.8 3.9 all-to-all-done.7
  269.0 4.8 %all-to-all-start.8 = ((bf16[8,192,128]{2,1,0:T(8,128)(2,1)}), bf16[8,192,128]{2,1,0:T(8,128)(2,1)S(1)}, u32[]{:S(2)}, u32[]{:S(2)}) async-start(bf16[8,192,128]{2,1,0:T(8,128)(2,1)} %bitcast.225), calls=%async_computation.8 | async-start | bytes 786432 | tf_op jit(solution)/shard_map/all_to_all | solution.py:51
  288.0 4.7 %all-to-all-start.9 = ((bf16[8,64,1024]{2,1,0:T(8,128)(2,1)}), bf16[8,64,1024]{2,1,0:T(8,128)(2,1)}, u32[]{:S(2)}, u32[]{:S(2)}) async-start(bf16[8,64,1024]{2,1,0:T(8,128)(2,1)} %fusion.6), calls=%async_computation.9 | async-start | bytes 2097152 | tf_op jit(solution)/shard_map/all_to_all | solution.py:51
  295.0 12.4 %attend_backward.1 = (bf16[1536,256]{1,0:T(8,128)(2,1)}, f32[64,256]{1,0:T(8,128)S(1)}) custom-call(s32[16]{0:T(128)S(1)} %bitcast.211, bf16[256,1536]{1,0:T(8,128)(2,1)S(1)} %get-tuple-element.77.cols_ref, bf16[1536,256]{1,0:T(8,128)(2,1)S(1)} %copy-done.4, bf16[1536,128]{1,0:T(8,128)(2,1)S(1)} %bitcast.207, f32[128,1536]{1,0:T(8,128)S(1)} %copy-done.6, ...), custom_call_target="tpu_custom_call" | custom-call | flops 10000000000 | bytes 8000000 | tf_op jit(solution)/shard_map/attend_backward/pallas_call | solution.py:267
  316.3 6.7 %all-to-all-start.10 = ((bf16[8,192,256]{2,1,0:T(8,128)(2,1)}), bf16[8,192,256]{2,1,0:T(8,128)(2,1)S(1)}, u32[]{:S(2)}, u32[]{:S(2)}) async-start(bf16[8,192,256]{2,1,0:T(8,128)(2,1)} %bitcast.40), calls=%async_computation.10 | async-start | bytes 1572864 | tf_op jit(solution)/shard_map/all_to_all | solution.py:51
  334.3 6.7 %all-to-all-start.11 = ((bf16[8,144,256]{2,1,0:T(8,128)(2,1)}), bf16[8,144,256]{2,1,0:T(8,128)(2,1)S(1)}, u32[]{:S(2)}, u32[]{:S(2)}) async-start(bf16[8,144,256]{2,1,0:T(8,128)(2,1)} %maximum_maximum_fusion), calls=%async_computation.11 | async-start | bytes 1179648 | tf_op jit(solution)/shard_map/all_to_all | solution.py:51
  346.5 6.0 %collective-permute-start.32 = (bf16[8,64,2048]{2,1,0:T(8,128)(2,1)}, bf16[8,64,2048]{2,1,0:T(8,128)(2,1)}, u32[]{:S(2)}, u32[]{:S(2)}) collective-permute-start(bf16[8,64,2048]{2,1,0:T(8,128)(2,1)} %all-to-all-done.5), channel_id=1, source_target_pairs={{0,8},{1,9},{2,10},{3,11},{4,12},{5,13},{6,14},{7,15},{8,0},{9,1},... | collective-permute-start | bytes 6291464 | tf_op jit(solution)/shard_map/ppermute | solution.py:47
  373.1 6.0 %all-to-all-done.12 = bf16[16,104,256]{2,1,0:T(8,128)(2,1)S(1)} async-done(((bf16[16,104,256]{2,1,0:T(8,128)(2,1)}), bf16[16,104,256]{2,1,0:T(8,128)(2,1)S(1)}, u32[]{:S(2)}, u32[]{:S(2)}) %all-to-all-start.12) | async-done | bytes 852000 | tf_op jit(solution)/shard_map/all_to_all | solution.py:538
  380.2 5.1 %all-to-all-start.13 = ((bf16[16,104,256]{2,1,0:T(8,128)(2,1)}), bf16[16,104,256]{2,1,0:T(8,128)(2,1)}, u32[]{:S(2)}, u32[]{:S(2)}) async-start(bf16[16,104,256]{2,1,0:T(8,128)(2,1)} %broadcast_in_dim.247), calls=%async_computation.13 | async-start | bytes 1703936 | tf_op jit(solution)/shard_map/all_to_all | solution.py:540
  388.5 4.5 %spread_slices.1 = (f32[128,4608]{1,0:T(8,128)}, f32[128,4608]{1,0:T(8,128)}, f32[576,1024]{1,0:T(8,128)}) custom-call(s32[5]{0:T(128)S(1)} %pad_add_fusion.index_ref, bf16[4,64,2304]{2,1,0:T(8,128)(2,1)S(1)} %pad_maximum_fusion.1.mine_ref, bf16[4,64,2304]{2,1,0:T(8,128)(2,1)S(1)} %collective-permute-done.33.other_ref, ...), custom_call_target="tpu_custom_call" | custom-call | flops 10000000 | bytes 10000000 | tf_op jit(solution)/shard_map/spread_slices/pallas_call | solution.py:313
  393.0 5.9 %all-to-all-done.13 = bf16[16,104,256]{2,1,0:T(8,128)(2,1)} async-done(((bf16[16,104,256]{2,1,0:T(8,128)(2,1)}), bf16[16,104,256]{2,1,0:T(8,128)(2,1)}, u32[]{:S(2)}, u32[]{:S(2)}) %all-to-all-start.13) | async-done | bytes 852000 | tf_op jit(solution)/shard_map/all_to_all | solution.py:540
  (319 shorter events, 193.8 us)
Async XLA Ops:
  7.2 84.8 %all-gather.3.cloned.1.call-start = ((), (), s32[]{:S(2)}) async-start(), calls=%async_computation.14 | async-start | bytes 3538944 | tf_op jit(solution)/shard_map/all_gather | solution.py:372
  7.9 65.2 %collective-permute-start.1 = (bf16[192,1024]{1,0:T(8,128)(2,1)}, bf16[192,1024]{1,0:T(8,128)(2,1)}, u32[]{:S(2)}, u32[]{:S(2)}) collective-permute-start(bf16[192,1024]{1,0:T(8,128)(2,1)} %bitcast.217), channel_id=1, source_target_pairs={{0,32},{1,33},{2,34},{3,35},{4,36},{5,37},{6,38},{7,39},{8,40},{9,... | collective-permute-start | bytes 1179656 | tf_op jit(solution)/shard_map/ppermute | solution.py:47
  10.0 64.1 %collective-permute-start.2 = (bf16[192,1024]{1,0:T(8,128)(2,1)}, bf16[192,1024]{1,0:T(8,128)(2,1)}, u32[]{:S(2)}, u32[]{:S(2)}) collective-permute-start(bf16[192,1024]{1,0:T(8,128)(2,1)} %bitcast.218), channel_id=1, source_target_pairs={{0,96},{1,97},{2,98},{3,99},{4,100},{5,101},{6,102},{7,103},{8,104... | collective-permute-start | bytes 1179656 | tf_op jit(solution)/shard_map/ppermute | solution.py:47
  18.1 20.7 %all-to-all-start = ((bf16[8,144,256]{2,1,0:T(8,128)(2,1)}), bf16[8,144,256]{2,1,0:T(8,128)(2,1)S(1)}, u32[]{:S(2)}, u32[]{:S(2)}) async-start(bf16[8,144,256]{2,1,0:T(8,128)(2,1)} %copy.125), calls=%async_computation | async-start | bytes 1179648 | tf_op jit(solution)/shard_map/all_to_all | solution.py:51
  39.8 20.4 %all-to-all-start.1 = ((bf16[8,64,1024]{2,1,0:T(8,128)(2,1)}), bf16[8,64,1024]{2,1,0:T(8,128)(2,1)S(1)}, u32[]{:S(2)}, u32[]{:S(2)}) async-start(bf16[8,64,1024]{2,1,0:T(8,128)(2,1)} %broadcast_in_dim.208), calls=%async_computation.1 | async-start | bytes 2097152 | tf_op jit(solution)/shard_map/all_to_all | solution.py:51
  64.6 24.6 %collective-permute-start = (bf16[8,64,1024]{2,1,0:T(8,128)(2,1)S(1)}, bf16[8,64,1024]{2,1,0:T(8,128)(2,1)}, u32[]{:S(2)}, u32[]{:S(2)}) collective-permute-start(bf16[8,64,1024]{2,1,0:T(8,128)(2,1)S(1)} %all-to-all-done.1), channel_id=1, source_target_pairs={{0,8},{1,9},{2,10},{3,11},{4,12},{5,13},{6,14},{7,15},{8,0},{9,1},... | collective-permute-start | bytes 3145736 | tf_op jit(solution)/shard_map/ppermute | solution.py:47
  74.1 13.7 %collective-permute-start.3 = (bf16[96,1024]{1,0:T(8,128)(2,1)S(1)}, bf16[96,1024]{1,0:T(8,128)(2,1)S(1)}, u32[]{:S(2)}, u32[]{:S(2)}) collective-permute-start(bf16[96,1024]{1,0:T(8,128)(2,1)S(1)} %slice.247), channel_id=1, source_target_pairs={{0,32},{1,33},{2,34},{3,35},{4,36},{5,37},{6,38},{7,39},{8,40},{9,... | collective-permute-start | bytes 589832 | tf_op jit(solution)/shard_map/ppermute | solution.py:47
  75.8 12.7 %collective-permute-start.4 = (bf16[96,1024]{1,0:T(8,128)(2,1)}, bf16[96,1024]{1,0:T(8,128)(2,1)S(1)}, u32[]{:S(2)}, u32[]{:S(2)}) collective-permute-start(bf16[96,1024]{1,0:T(8,128)(2,1)} %slice.248), channel_id=1, source_target_pairs={{0,96},{1,97},{2,98},{3,99},{4,100},{5,101},{6,102},{7,103},{8,104... | collective-permute-start | bytes 589832 | tf_op jit(solution)/shard_map/ppermute | solution.py:47
  82.2 20.5 %all-to-all-start.2 = ((bf16[8,72,1024]{2,1,0:T(8,128)(2,1)}), bf16[8,72,1024]{2,1,0:T(8,128)(2,1)}, u32[]{:S(2)}, u32[]{:S(2)}) async-start(bf16[8,72,1024]{2,1,0:T(8,128)(2,1)} %broadcast_in_dim.219), calls=%async_computation.2 | async-start | bytes 2359296 | tf_op jit(solution)/shard_map/all_to_all | solution.py:51
  117.1 35.7 %all-to-all-start.4 = ((bf16[8,64,2304]{2,1,0:T(8,128)(2,1)}), bf16[8,64,2304]{2,1,0:T(8,128)(2,1)}, u32[]{:S(2)}, u32[]{:S(2)}) async-start(bf16[8,64,2304]{2,1,0:T(8,128)(2,1)} %broadcast_in_dim.217), calls=%async_computation.4 | async-start | bytes 4718592 | tf_op jit(solution)/shard_map/all_to_all | solution.py:51
  121.6 27.9 %collective-permute-start.9 = (bf16[8,72,1024]{2,1,0:T(8,128)(2,1)}, bf16[8,72,1024]{2,1,0:T(8,128)(2,1)}, u32[]{:S(2)}, u32[]{:S(2)}) collective-permute-start(bf16[8,72,1024]{2,1,0:T(8,128)(2,1)} %all-to-all-done.2), channel_id=1, source_target_pairs={{0,8},{1,9},{2,10},{3,11},{4,12},{5,13},{6,14},{7,15},{8,0},{9,1},... | collective-permute-start | bytes 3538952 | tf_op jit(solution)/shard_map/ppermute | solution.py:47
  128.8 12.3 %collective-permute-start.6 = (bf16[192,1024]{1,0:T(8,128)(2,1)}, bf16[192,1024]{1,0:T(8,128)(2,1)}, u32[]{:S(2)}, u32[]{:S(2)}) collective-permute-start(bf16[192,1024]{1,0:T(8,128)(2,1)} %get-tuple-element.150), channel_id=1, source_target_pairs={{0,96},{1,97},{2,98},{3,99},{4,100},{5,101},{6,102},{7,103},{8,104... | collective-permute-start | bytes 1179656 | tf_op jit(solution)/shard_map/ppermute | solution.py:47
  154.3 33.6 %all-to-all-start.5 = ((bf16[8,64,2048]{2,1,0:T(8,128)(2,1)}), bf16[8,64,2048]{2,1,0:T(8,128)(2,1)}, u32[]{:S(2)}, u32[]{:S(2)}) async-start(bf16[8,64,2048]{2,1,0:T(8,128)(2,1)} %broadcast_in_dim.220), calls=%async_computation.5 | async-start | bytes 4194304 | tf_op jit(solution)/shard_map/all_to_all | solution.py:51
  197.2 15.8 %collective-permute-start.12 = (bf16[8,64,2304]{2,1,0:T(8,128)(2,1)}, bf16[8,64,2304]{2,1,0:T(8,128)(2,1)}, u32[]{:S(2)}, u32[]{:S(2)}) collective-permute-start(bf16[8,64,2304]{2,1,0:T(8,128)(2,1)} %dynamic-slice_bitcast_fusion), channel_id=1, source_target_pairs={{0,8},{1,9},{2,10},{3,11},{4,12},{5,13},{6,14},{7,15},{8,0},{9,1},... | collective-permute-start | bytes 7077896 | tf_op jit(solution)/shard_map/ppermute | solution.py:47
  198.4 21.5 %all-to-all-start.6 = ((bf16[8,72,1024]{2,1,0:T(8,128)(2,1)}), bf16[8,72,1024]{2,1,0:T(8,128)(2,1)}, u32[]{:S(2)}, u32[]{:S(2)}) async-start(bf16[8,72,1024]{2,1,0:T(8,128)(2,1)} %fusion.5), calls=%async_computation.6 | async-start | bytes 2359296 | tf_op jit(solution)/shard_map/all_to_all | solution.py:51
  219.8 34.8 %all-to-all-start.7 = ((bf16[8,64,2304]{2,1,0:T(8,128)(2,1)}), bf16[8,64,2304]{2,1,0:T(8,128)(2,1)}, u32[]{:S(2)}, u32[]{:S(2)}) async-start(bf16[8,64,2304]{2,1,0:T(8,128)(2,1)} %fusion), calls=%async_computation.7 | async-start | bytes 4718592 | tf_op jit(solution)/shard_map/all_to_all | solution.py:51
  254.7 19.1 %collective-permute-start.19 = (bf16[72,1024]{1,0:T(8,128)(2,1)S(1)}, bf16[72,1024]{1,0:T(8,128)(2,1)}, u32[]{:S(2)}, u32[]{:S(2)}) collective-permute-start(bf16[72,1024]{1,0:T(8,128)(2,1)S(1)} %reduce_sum.130), channel_id=1, source_target_pairs={{0,16},{1,17},{2,18},{3,19},{4,20},{5,21},{6,22},{7,23},{8,24},{9,... | collective-permute-start | bytes 442376 | tf_op jit(solution)/shard_map/ppermute | solution.py:47
  263.3 14.8 %collective-permute-start.17 = (bf16[8,64,1024]{2,1,0:T(8,128)(2,1)}, bf16[8,64,1024]{2,1,0:T(8,128)(2,1)}, u32[]{:S(2)}, u32[]{:S(2)}) collective-permute-start(bf16[8,64,1024]{2,1,0:T(8,128)(2,1)} %dynamic-slice_bitcast_fusion.2), channel_id=1, source_target_pairs={{0,8},{1,9},{2,10},{3,11},{4,12},{5,13},{6,14},{7,15},{8,0},{9,1},... | collective-permute-start | bytes 3145736 | tf_op jit(solution)/shard_map/ppermute | solution.py:47
  269.0 13.1 %all-to-all-start.8 = ((bf16[8,192,128]{2,1,0:T(8,128)(2,1)}), bf16[8,192,128]{2,1,0:T(8,128)(2,1)S(1)}, u32[]{:S(2)}, u32[]{:S(2)}) async-start(bf16[8,192,128]{2,1,0:T(8,128)(2,1)} %bitcast.225), calls=%async_computation.8 | async-start | bytes 786432 | tf_op jit(solution)/shard_map/all_to_all | solution.py:51
  282.1 28.6 %collective-permute-start.24 = (bf16[72,1024]{1,0:T(8,128)(2,1)}, bf16[72,1024]{1,0:T(8,128)(2,1)}, u32[]{:S(2)}, u32[]{:S(2)}) collective-permute-start(bf16[72,1024]{1,0:T(8,128)(2,1)} %add_convert_fusion.6), channel_id=1, source_target_pairs={{0,32},{1,33},{2,34},{3,35},{4,36},{5,37},{6,38},{7,39},{8,40},{9,... | collective-permute-start | bytes 442376 | tf_op jit(solution)/shard_map/ppermute | solution.py:47
  282.5 29.2 %collective-permute-start.25 = (bf16[72,1024]{1,0:T(8,128)(2,1)}, bf16[72,1024]{1,0:T(8,128)(2,1)}, u32[]{:S(2)}, u32[]{:S(2)}) collective-permute-start(bf16[72,1024]{1,0:T(8,128)(2,1)} %add_convert_fusion.6), channel_id=1, source_target_pairs={{0,96},{1,97},{2,98},{3,99},{4,100},{5,101},{6,102},{7,103},{8,104... | collective-permute-start | bytes 442376 | tf_op jit(solution)/shard_map/ppermute | solution.py:47
  285.1 37.9 %collective-permute-start.20 = (bf16[64,2304]{1,0:T(8,128)(2,1)}, bf16[64,2304]{1,0:T(8,128)(2,1)}, u32[]{:S(2)}, u32[]{:S(2)}) collective-permute-start(bf16[64,2304]{1,0:T(8,128)(2,1)} %add_convert_fusion.1), channel_id=1, source_target_pairs={{0,32},{1,33},{2,34},{3,35},{4,36},{5,37},{6,38},{7,39},{8,40},{9,... | collective-permute-start | bytes 884744 | tf_op jit(solution)/shard_map/ppermute | solution.py:47
  285.1 38.9 %collective-permute-start.21 = (bf16[64,2304]{1,0:T(8,128)(2,1)}, bf16[64,2304]{1,0:T(8,128)(2,1)}, u32[]{:S(2)}, u32[]{:S(2)}) collective-permute-start(bf16[64,2304]{1,0:T(8,128)(2,1)} %add_convert_fusion.1), channel_id=1, source_target_pairs={{0,96},{1,97},{2,98},{3,99},{4,100},{5,101},{6,102},{7,103},{8,104... | collective-permute-start | bytes 884744 | tf_op jit(solution)/shard_map/ppermute | solution.py:47
  288.0 28.3 %all-to-all-start.9 = ((bf16[8,64,1024]{2,1,0:T(8,128)(2,1)}), bf16[8,64,1024]{2,1,0:T(8,128)(2,1)}, u32[]{:S(2)}, u32[]{:S(2)}) async-start(bf16[8,64,1024]{2,1,0:T(8,128)(2,1)} %fusion.6), calls=%async_computation.9 | async-start | bytes 2097152 | tf_op jit(solution)/shard_map/all_to_all | solution.py:51
  316.3 18.0 %all-to-all-start.10 = ((bf16[8,192,256]{2,1,0:T(8,128)(2,1)}), bf16[8,192,256]{2,1,0:T(8,128)(2,1)S(1)}, u32[]{:S(2)}, u32[]{:S(2)}) async-start(bf16[8,192,256]{2,1,0:T(8,128)(2,1)} %bitcast.40), calls=%async_computation.10 | async-start | bytes 1572864 | tf_op jit(solution)/shard_map/all_to_all | solution.py:51
  334.3 19.2 %all-to-all-start.11 = ((bf16[8,144,256]{2,1,0:T(8,128)(2,1)}), bf16[8,144,256]{2,1,0:T(8,128)(2,1)S(1)}, u32[]{:S(2)}, u32[]{:S(2)}) async-start(bf16[8,144,256]{2,1,0:T(8,128)(2,1)} %maximum_maximum_fusion), calls=%async_computation.11 | async-start | bytes 1179648 | tf_op jit(solution)/shard_map/all_to_all | solution.py:51
  343.1 27.1 %collective-permute-start.29 = (bf16[192,1024]{1,0:T(8,128)(2,1)}, bf16[192,1024]{1,0:T(8,128)(2,1)}, u32[]{:S(2)}, u32[]{:S(2)}) collective-permute-start(bf16[192,1024]{1,0:T(8,128)(2,1)} %pad_maximum_fusion.7), channel_id=1, source_target_pairs={{0,32},{1,33},{2,34},{3,35},{4,36},{5,37},{6,38},{7,39},{8,40},{9,... | collective-permute-start | bytes 1179656 | tf_op jit(solution)/shard_map/ppermute | solution.py:47
  343.9 26.3 %collective-permute-start.31 = (bf16[192,1024]{1,0:T(8,128)(2,1)}, bf16[192,1024]{1,0:T(8,128)(2,1)}, u32[]{:S(2)}, u32[]{:S(2)}) collective-permute-start(bf16[192,1024]{1,0:T(8,128)(2,1)} %pad_maximum_fusion.8), channel_id=1, source_target_pairs={{0,96},{1,97},{2,98},{3,99},{4,100},{5,101},{6,102},{7,103},{8,104... | collective-permute-start | bytes 1179656 | tf_op jit(solution)/shard_map/ppermute | solution.py:47
  346.5 19.2 %collective-permute-start.32 = (bf16[8,64,2048]{2,1,0:T(8,128)(2,1)}, bf16[8,64,2048]{2,1,0:T(8,128)(2,1)}, u32[]{:S(2)}, u32[]{:S(2)}) collective-permute-start(bf16[8,64,2048]{2,1,0:T(8,128)(2,1)} %all-to-all-done.5), channel_id=1, source_target_pairs={{0,8},{1,9},{2,10},{3,11},{4,12},{5,13},{6,14},{7,15},{8,0},{9,1},... | collective-permute-start | bytes 6291464 | tf_op jit(solution)/shard_map/ppermute | solution.py:47
  354.7 33.8 %collective-permute-start.33 = (bf16[4,64,2304]{2,1,0:T(8,128)(2,1)S(1)}, bf16[4,64,2304]{2,1,0:T(8,128)(2,1)S(1)}, u32[]{:S(2)}, u32[]{:S(2)}) collective-permute-start(bf16[4,64,2304]{2,1,0:T(8,128)(2,1)S(1)} %pad_maximum_fusion.1.mine_ref), channel_id=1, source_target_pairs={{0,8},{1,9},{2,10},{3,11},{4,12},{5,13},{6,14},{7,15},{8,0},{9,1},... | collective-permute-start | bytes 3538952 | tf_op jit(solution)/shard_map/ppermute | solution.py:47
  362.0 17.0 %all-to-all-start.12 = ((bf16[16,104,256]{2,1,0:T(8,128)(2,1)}), bf16[16,104,256]{2,1,0:T(8,128)(2,1)S(1)}, u32[]{:S(2)}, u32[]{:S(2)}) async-start(bf16[16,104,256]{2,1,0:T(8,128)(2,1)} %fusion.25), calls=%async_computation.12 | async-start | bytes 1703936 | tf_op jit(solution)/shard_map/all_to_all | solution.py:538
  380.2 18.7 %all-to-all-start.13 = ((bf16[16,104,256]{2,1,0:T(8,128)(2,1)}), bf16[16,104,256]{2,1,0:T(8,128)(2,1)}, u32[]{:S(2)}, u32[]{:S(2)}) async-start(bf16[16,104,256]{2,1,0:T(8,128)(2,1)} %broadcast_in_dim.247), calls=%async_computation.13 | async-start | bytes 1703936 | tf_op jit(solution)/shard_map/all_to_all | solution.py:540
  (63 other events, 735.0 us)
Sparse Core Ops, SparseCore 0:
  10.3 74.6 all-gather.2

commit v2 on v1

--- a/solution.py
+++ b/solution.py
@@ -505,7 +505,6 @@
     )
     qkv_sent, packed, qkv_half = tie(qkv_sent, packed, qkv_half)
     qkv_got = exchange_grp(qkv_sent)
-    qkv_got, gate_up_parts, down_parts = tie(qkv_got, gate_up_parts, down_parts)
     grad_packed = packed.transpose(1, 0, 2)
     qkv_rows = qkv_got[:, :128]
     out_sum = jnp.sum(out_got.astype(F32), axis=0).astype(BF16)
@@ -535,7 +534,9 @@
         + [gain_columns.reshape(16, 8, 256)],
         axis=1,
     )
-    rep_got, outputs = tie(lax.all_to_all(attn_rows, "rep", 0, 0), outputs)
+    rep_got, outputs, gate_up_parts, down_parts = tie(
+        lax.all_to_all(attn_rows, "rep", 0, 0), outputs, gate_up_parts, down_parts
+    )
     attn_part = jnp.sum(rep_got.astype(F32), axis=0).astype(BF16)
     attn_all = lax.all_to_all(
         jnp.broadcast_to(attn_part[None], (16, 104, 256)), "rep", 0, 0

time: 421 us -> 431 us (1.024)
  local copies, waits for them, and re-layouts: 65.7 us -> 70.1 us
    convert_element_type x4, local copies, waits for them, and re-layouts: 1.92 us -> 6.63 us  [by_head(): return cut.reshape(128, 8 * width).astype(F32)]
    all_to_all x1, starting transfers between devices: 3.64 us -> 8.07 us  [per_device(): lax.all_to_all(attn_rows, 'rep', 0, 0)]
    unnamed x110 -> x100, local copies, waits for them, and re-layouts: 31 us -> 32.2 us
  transfers between devices with their start and end apart: 49 -> 49, of which waited for: 15 -> 14; matrix products, arithmetic and copies ran while one was open for 34% -> 36% of each run, Pallas kernels for 6% -> 5%
where the time goes in v2:
time: 431 us; the launch traced here: 424 us
  starting transfers between devices  133 us (31%)
  local copies, waits for them, and re-layouts  70.1 us (16%)
  other arithmetic  66.4 us (15%)
  waiting for transfers between devices  59.7 us (14%)
  matrix products  38.2 us (9%)
  Pallas kernels  26 us (6%)
  between operations  15.4 us (4%)
  blocking collectives  14.4 us (3%)
    all_to_all x11, starting transfers between devices, exchange_grp(): return lax.all_to_all(value, 'grp', 0, 0)  61.4 us
    ppermute x35, starting transfers between devices, send(): return lax.ppermute(value, AXES, perm)  59.2 us
    unnamed x100, local copies, waits for them, and re-layouts  32.2 us
    all_to_all x11, waiting for transfers between devices, exchange_grp(): return lax.all_to_all(value, 'grp', 0, 0)  25.3 us
    ppermute x35, waiting for transfers between devices, send(): return lax.ppermute(value, AXES, perm)  17.9 us
    all_to_all x1, blocking collectives, exchange_grp(): return lax.all_to_all(value, 'grp', 0, 0)  14.4 us
    pallas_call x1, Pallas kernels, attend_backward(): pl.pallas_call(backward_kernel, out_shape=(jax.ShapeDtypeStruct((SEQ, 256...  12.4 us
    select_n x4, other arithmetic, both_cores(): jnp.where(picked, mine[:, None], other[:, None]).reshape(-1, mine.shape[-1])  11.7 us
  transfers between devices with their start and end apart: 49, of which 14 were waited for; matrix products, arithmetic and copies ran while one was open for 36% of the time, Pallas kernels for 5%

profile of v2, /device:TPU:1, one launch (start us, length us, event | category | flops | bytes accessed | tf_op | source)
XLA Modules:
  0.0 423.5 jit_solution(15668664375610799537)
XLA Ops:
  18.5 7.8 %all-to-all-start = ((bf16[8,144,256]{2,1,0:T(8,128)(2,1)}), bf16[8,144,256]{2,1,0:T(8,128)(2,1)S(1)}, u32[]{:S(2)}, u32[]{:S(2)}) async-start(bf16[8,144,256]{2,1,0:T(8,128)(2,1)} %copy.125), calls=%async_computation | async-start | bytes 1179648 | tf_op jit(solution)/shard_map/all_to_all | solution.py:51
  33.2 5.5 %all-to-all-done = bf16[8,144,256]{2,1,0:T(8,128)(2,1)S(1)} async-done(((bf16[8,144,256]{2,1,0:T(8,128)(2,1)}), bf16[8,144,256]{2,1,0:T(8,128)(2,1)S(1)}, u32[]{:S(2)}, u32[]{:S(2)}) %all-to-all-start) | async-done | bytes 589856 | tf_op jit(solution)/shard_map/all_to_all | solution.py:51
  39.8 4.0 all-to-all-start.1
  48.2 10.4 %all-to-all-done.1 = bf16[8,64,1024]{2,1,0:T(8,128)(2,1)S(1)} async-done(((bf16[8,64,1024]{2,1,0:T(8,128)(2,1)}), bf16[8,64,1024]{2,1,0:T(8,128)(2,1)S(1)}, u32[]{:S(2)}, u32[]{:S(2)}) %all-to-all-start.1) | async-done | bytes 1048608 | tf_op jit(solution)/shard_map/all_to_all | solution.py:51
  62.9 9.2 %collective-permute-start = (bf16[8,64,1024]{2,1,0:T(8,128)(2,1)S(1)}, bf16[8,64,1024]{2,1,0:T(8,128)(2,1)}, u32[]{:S(2)}, u32[]{:S(2)}) collective-permute-start(bf16[8,64,1024]{2,1,0:T(8,128)(2,1)S(1)} %all-to-all-done.1), channel_id=1, source_target_pairs={{0,8},{1,9},{2,10},{3,11},{4,12},{5,13},{6,14},{7,15},{8,0},{9,1},... | collective-permute-start | bytes 3145736 | tf_op jit(solution)/shard_map/ppermute | solution.py:47
  82.1 4.5 %all-to-all-start.2 = ((bf16[8,72,1024]{2,1,0:T(8,128)(2,1)}), bf16[8,72,1024]{2,1,0:T(8,128)(2,1)}, u32[]{:S(2)}, u32[]{:S(2)}) async-start(bf16[8,72,1024]{2,1,0:T(8,128)(2,1)} %broadcast_in_dim.219), calls=%async_computation.2 | async-start | bytes 2359296 | tf_op jit(solution)/shard_map/all_to_all | solution.py:51
  91.8 8.4 %attend_forward.1 = (bf16[1536,128]{1,0:T(8,128)(2,1)S(1)}, bf16[1536,1024]{1,0:T(8,128)(2,1)}, bf16[256,1536]{1,0:T(8,128)(2,1)S(1)}, bf16[1536,256]{1,0:T(8,12...) custom-call(s32[16]{0:T(128)S(1)} %bitcast.210, ...), custom_call_target="tpu_custom_call" | custom-call | flops 6000000000 | bytes 14000000 | tf_op jit(solution)/shard_map/attend_forward/pallas_call | solution.py:176
  102.6 14.4 %all_to_all.70 = bf16[8,192,128]{2,1,0:T(8,128)(2,1)} all-to-all(bf16[8,192,128]{2,1,0:T(8,128)(2,1)S(1)} %bitcast.208), channel_id=1, replica_groups=mesh['rep'=16,'grp'=8] {'grp'}, dimensions={0} | all-to-all | bytes 786432 | tf_op jit(solution)/shard_map/all_to_all | solution.py:51
  117.0 4.5 %all-to-all-start.4 = ((bf16[8,64,2304]{2,1,0:T(8,128)(2,1)}), bf16[8,64,2304]{2,1,0:T(8,128)(2,1)}, u32[]{:S(2)}, u32[]{:S(2)}) async-start(bf16[8,64,2304]{2,1,0:T(8,128)(2,1)} %broadcast_in_dim.217), calls=%async_computation.4 | async-start | bytes 4718592 | tf_op jit(solution)/shard_map/all_to_all | solution.py:51
  131.5 9.4 %collective-permute-done.5 = bf16[192,1024]{1,0:T(8,128)(2,1)S(1)} collective-permute-done((bf16[192,1024]{1,0:T(8,128)(2,1)}, bf16[192,1024]{1,0:T(8,128)(2,1)S(1)}, u32[]{:S(2)}, u32[]{:S(2)}) %collective-permute-start.5) | collective-permute-done | bytes 393248 | tf_op jit(solution)/shard_map/ppermute | solution.py:47
  154.2 7.2 %all-to-all-start.5 = ((bf16[8,64,2048]{2,1,0:T(8,128)(2,1)}), bf16[8,64,2048]{2,1,0:T(8,128)(2,1)}, u32[]{:S(2)}, u32[]{:S(2)}) async-start(bf16[8,64,2048]{2,1,0:T(8,128)(2,1)} %broadcast_in_dim.220), calls=%async_computation.5 | async-start | bytes 4194304 | tf_op jit(solution)/shard_map/all_to_all | solution.py:51
  166.6 3.8 fusion.39
  170.4 5.0 %fusion.3 = (bf16[768,1152]{1,0:T(8,128)(2,1)}, bf16[768,1152]{1,0:T(8,128)(2,1)}, bf16[768,1152]{1,0:T(8,128)(2,1)S(1)}) fusion(f32[768,2304]{1,0:T(8,128)S(1)} %fusion.39, bf16[768,1024]{1,0:T(8,128)(2,1)S(1)} %copy-done.31, bf16[1152,1024]{1,0:T(8,128)(2,1)S(1)} %copy-done.24), kind=kOutput, calls=%fused_computation.10 | convolution fusion | flops 1826095104 | bytes 16318464 | tf_op jit(solution)/shard_map/td,fd->tf/dot_general | solution.py:439
  180.3 4.3 %pad_maximum_fusion = bf16[768,2304]{1,0:T(8,128)(2,1)} fusion(bf16[768,1152]{1,0:T(8,128)(2,1)} %get-tuple-element.150, bf16[768,1152]{1,0:T(8,128)(2,1)} %get-tuple-element.149), kind=kLoop, calls=%fused_computation.11 | loop fusion | flops 7077888 | bytes 7077888 | tf_op jit(solution)/shard_map/concatenate | solution.py:441
  187.8 6.4 %convolution_convert_fusion = bf16[1024,2304]{1,0:T(8,128)(2,1)S(1)} fusion(bf16[768,1024]{1,0:T(8,128)(2,1)} %constant_dynamic-update-slice_fusion.5, bf16[768,2304]{1,0:T(8,128)(2,1)} %pad_maximum_fusion), kind=kOutput, calls=%fused_computation.1 | convolution fusion | flops 3626237952 | bytes 9830400 | tf_op jit(solution)/shard_map/td,tf->df/dot_general | solution.py:444
  198.3 5.6 %all-to-all-start.6 = ((bf16[8,72,1024]{2,1,0:T(8,128)(2,1)}), bf16[8,72,1024]{2,1,0:T(8,128)(2,1)}, u32[]{:S(2)}, u32[]{:S(2)}) async-start(bf16[8,72,1024]{2,1,0:T(8,128)(2,1)} %fusion.5), calls=%async_computation.6 | async-start | bytes 2359296 | tf_op jit(solution)/shard_map/all_to_all | solution.py:51
  203.9 9.0 %fusion.40 = f32[768,1024]{1,0:T(8,128)} fusion(bf16[768,2304]{1,0:T(8,128)(2,1)} %pad_maximum_fusion, bf16[1024,2304]{1,0:T(8,128)(2,1)} %copy-done.16), kind=kOutput, calls=%fused_computation.162 | convolution fusion | flops 3623878656 | bytes 11403264 | tf_op jit(solution)/shard_map/tf,df->td/dot_general | solution.py:446
  219.8 5.7 %all-to-all-start.7 = ((bf16[8,64,2304]{2,1,0:T(8,128)(2,1)}), bf16[8,64,2304]{2,1,0:T(8,128)(2,1)}, u32[]{:S(2)}, u32[]{:S(2)}) async-start(bf16[8,64,2304]{2,1,0:T(8,128)(2,1)} %fusion), calls=%async_computation.7 | async-start | bytes 4718592 | tf_op jit(solution)/shard_map/all_to_all | solution.py:51
  230.9 4.5 %collective-permute-done.13 = bf16[96,1024]{1,0:T(8,128)(2,1)S(1)} collective-permute-done((bf16[96,1024]{1,0:T(8,128)(2,1)S(1)}, bf16[96,1024]{1,0:T(8,128)(2,1)S(1)}, u32[]{:S(2)}, u32[]{:S(2)}) %collective-permute-start.13) | collective-permute-done | bytes 196640 | tf_op jit(solution)/shard_map/ppermute | solution.py:47
  240.9 3.9 fusion.41
  250.7 3.9 all-to-all-done.7
  269.7 4.5 %all-to-all-start.8 = ((bf16[8,192,128]{2,1,0:T(8,128)(2,1)}), bf16[8,192,128]{2,1,0:T(8,128)(2,1)S(1)}, u32[]{:S(2)}, u32[]{:S(2)}) async-start(bf16[8,192,128]{2,1,0:T(8,128)(2,1)} %bitcast.225), calls=%async_computation.8 | async-start | bytes 786432 | tf_op jit(solution)/shard_map/all_to_all | solution.py:51
  288.9 4.3 %all-to-all-start.9 = ((bf16[8,64,1024]{2,1,0:T(8,128)(2,1)}), bf16[8,64,1024]{2,1,0:T(8,128)(2,1)}, u32[]{:S(2)}, u32[]{:S(2)}) async-start(bf16[8,64,1024]{2,1,0:T(8,128)(2,1)} %fusion.6), calls=%async_computation.9 | async-start | bytes 2097152 | tf_op jit(solution)/shard_map/all_to_all | solution.py:51
  295.5 12.4 %attend_backward.1 = (bf16[1536,256]{1,0:T(8,128)(2,1)}, f32[64,256]{1,0:T(8,128)S(1)}) custom-call(s32[16]{0:T(128)S(1)} %bitcast.211, bf16[256,1536]{1,0:T(8,128)(2,1)S(1)} %get-tuple-element.76.cols_ref, bf16[1536,256]{1,0:T(8,128)(2,1)S(1)} %copy-done.4, bf16[1536,128]{1,0:T(8,128)(2,1)S(1)} %bitcast.207, f32[128,1536]{1,0:T(8,128)S(1)} %copy-done.6, ...), custom_call_target="tpu_custom_call" | custom-call | flops 10000000000 | bytes 8000000 | tf_op jit(solution)/shard_map/attend_backward/pallas_call | solution.py:267
  316.8 6.7 %all-to-all-start.10 = ((bf16[8,192,256]{2,1,0:T(8,128)(2,1)}), bf16[8,192,256]{2,1,0:T(8,128)(2,1)S(1)}, u32[]{:S(2)}, u32[]{:S(2)}) async-start(bf16[8,192,256]{2,1,0:T(8,128)(2,1)} %bitcast.40), calls=%async_computation.10 | async-start | bytes 1572864 | tf_op jit(solution)/shard_map/all_to_all | solution.py:51
  335.5 6.7 %all-to-all-start.11 = ((bf16[8,144,256]{2,1,0:T(8,128)(2,1)}), bf16[8,144,256]{2,1,0:T(8,128)(2,1)S(1)}, u32[]{:S(2)}, u32[]{:S(2)}) async-start(bf16[8,144,256]{2,1,0:T(8,128)(2,1)} %maximum_maximum_fusion), calls=%async_computation.11 | async-start | bytes 1179648 | tf_op jit(solution)/shard_map/all_to_all | solution.py:51
  347.7 5.9 %collective-permute-start.32 = (bf16[8,64,2048]{2,1,0:T(8,128)(2,1)}, bf16[8,64,2048]{2,1,0:T(8,128)(2,1)}, u32[]{:S(2)}, u32[]{:S(2)}) collective-permute-start(bf16[8,64,2048]{2,1,0:T(8,128)(2,1)} %all-to-all-done.5), channel_id=1, source_target_pairs={{0,8},{1,9},{2,10},{3,11},{4,12},{5,13},{6,14},{7,15},{8,0},{9,1},... | collective-permute-start | bytes 6291464 | tf_op jit(solution)/shard_map/ppermute | solution.py:47
  357.9 8.1 %all-to-all-start.12 = ((bf16[16,104,256]{2,1,0:T(8,128)(2,1)}), bf16[16,104,256]{2,1,0:T(8,128)(2,1)S(1)}, u32[]{:S(2)}, u32[]{:S(2)}) async-start(bf16[16,104,256]{2,1,0:T(8,128)(2,1)} %fusion.25), calls=%async_computation.12 | async-start | bytes 1703936 | tf_op jit(solution)/shard_map/all_to_all | solution.py:538
  373.2 6.2 %all-to-all-done.12 = bf16[16,104,256]{2,1,0:T(8,128)(2,1)S(1)} async-done(((bf16[16,104,256]{2,1,0:T(8,128)(2,1)}), bf16[16,104,256]{2,1,0:T(8,128)(2,1)S(1)}, u32[]{:S(2)}, u32[]{:S(2)}) %all-to-all-start.12) | async-done | bytes 852000 | tf_op jit(solution)/shard_map/all_to_all | solution.py:538
  380.5 4.5 %all-to-all-start.13 = ((bf16[16,104,256]{2,1,0:T(8,128)(2,1)}), bf16[16,104,256]{2,1,0:T(8,128)(2,1)S(1)}, u32[]{:S(2)}, u32[]{:S(2)}) async-start(bf16[16,104,256]{2,1,0:T(8,128)(2,1)} %broadcast_in_dim.247), calls=%async_computation.13 | async-start | bytes 1703936 | tf_op jit(solution)/shard_map/all_to_all | solution.py:541
  388.8 9.7 %all-to-all-done.13 = bf16[16,104,256]{2,1,0:T(8,128)(2,1)S(1)} async-done(((bf16[16,104,256]{2,1,0:T(8,128)(2,1)}), bf16[16,104,256]{2,1,0:T(8,128)(2,1)S(1)}, u32[]{:S(2)}, u32[]{:S(2)}) %all-to-all-start.13) | async-done | bytes 852000 | tf_op jit(solution)/shard_map/all_to_all | solution.py:541
  411.0 5.2 %spread_slices.1 = (f32[128,4608]{1,0:T(8,128)}, f32[128,4608]{1,0:T(8,128)}, f32[576,1024]{1,0:T(8,128)}) custom-call(s32[5]{0:T(128)S(1)} %pad_add_fusion.index_ref, bf16[4,64,2304]{2,1,0:T(8,128)(2,1)S(1)} %pad_maximum_fusion.1.mine_ref, bf16[4,64,2304]{2,1,0:T(8,128)(2,1)} %collective-permute-done.33.other_ref, ...), custom_call_target="tpu_custom_call" | custom-call | flops 10000000 | bytes 10000000 | tf_op jit(solution)/shard_map/spread_slices/pallas_call | solution.py:313
  (309 shorter events, 196.7 us)
Async XLA Ops:
  7.2 84.6 %all-gather.3.cloned.1.call-start = ((), (), s32[]{:S(2)}) async-start(), calls=%async_computation.14 | async-start | bytes 3538944 | tf_op jit(solution)/shard_map/all_gather | solution.py:372
  7.9 65.1 %collective-permute-start.1 = (bf16[192,1024]{1,0:T(8,128)(2,1)}, bf16[192,1024]{1,0:T(8,128)(2,1)}, u32[]{:S(2)}, u32[]{:S(2)}) collective-permute-start(bf16[192,1024]{1,0:T(8,128)(2,1)} %bitcast.217), channel_id=1, source_target_pairs={{0,32},{1,33},{2,34},{3,35},{4,36},{5,37},{6,38},{7,39},{8,40},{9,... | collective-permute-start | bytes 1179656 | tf_op jit(solution)/shard_map/ppermute | solution.py:47
  10.0 65.0 %collective-permute-start.2 = (bf16[192,1024]{1,0:T(8,128)(2,1)}, bf16[192,1024]{1,0:T(8,128)(2,1)}, u32[]{:S(2)}, u32[]{:S(2)}) collective-permute-start(bf16[192,1024]{1,0:T(8,128)(2,1)} %bitcast.218), channel_id=1, source_target_pairs={{0,96},{1,97},{2,98},{3,99},{4,100},{5,101},{6,102},{7,103},{8,104... | collective-permute-start | bytes 1179656 | tf_op jit(solution)/shard_map/ppermute | solution.py:47
  18.5 20.3 %all-to-all-start = ((bf16[8,144,256]{2,1,0:T(8,128)(2,1)}), bf16[8,144,256]{2,1,0:T(8,128)(2,1)S(1)}, u32[]{:S(2)}, u32[]{:S(2)}) async-start(bf16[8,144,256]{2,1,0:T(8,128)(2,1)} %copy.125), calls=%async_computation | async-start | bytes 1179648 | tf_op jit(solution)/shard_map/all_to_all | solution.py:51
  39.8 18.7 %all-to-all-start.1 = ((bf16[8,64,1024]{2,1,0:T(8,128)(2,1)}), bf16[8,64,1024]{2,1,0:T(8,128)(2,1)S(1)}, u32[]{:S(2)}, u32[]{:S(2)}) async-start(bf16[8,64,1024]{2,1,0:T(8,128)(2,1)} %broadcast_in_dim.208), calls=%async_computation.1 | async-start | bytes 2097152 | tf_op jit(solution)/shard_map/all_to_all | solution.py:51
  62.9 26.1 %collective-permute-start = (bf16[8,64,1024]{2,1,0:T(8,128)(2,1)S(1)}, bf16[8,64,1024]{2,1,0:T(8,128)(2,1)}, u32[]{:S(2)}, u32[]{:S(2)}) collective-permute-start(bf16[8,64,1024]{2,1,0:T(8,128)(2,1)S(1)} %all-to-all-done.1), channel_id=1, source_target_pairs={{0,8},{1,9},{2,10},{3,11},{4,12},{5,13},{6,14},{7,15},{8,0},{9,1},... | collective-permute-start | bytes 3145736 | tf_op jit(solution)/shard_map/ppermute | solution.py:47
  74.0 13.7 %collective-permute-start.3 = (bf16[96,1024]{1,0:T(8,128)(2,1)S(1)}, bf16[96,1024]{1,0:T(8,128)(2,1)S(1)}, u32[]{:S(2)}, u32[]{:S(2)}) collective-permute-start(bf16[96,1024]{1,0:T(8,128)(2,1)S(1)} %slice.247), channel_id=1, source_target_pairs={{0,32},{1,33},{2,34},{3,35},{4,36},{5,37},{6,38},{7,39},{8,40},{9,... | collective-permute-start | bytes 589832 | tf_op jit(solution)/shard_map/ppermute | solution.py:47
  82.1 20.5 %all-to-all-start.2 = ((bf16[8,72,1024]{2,1,0:T(8,128)(2,1)}), bf16[8,72,1024]{2,1,0:T(8,128)(2,1)}, u32[]{:S(2)}, u32[]{:S(2)}) async-start(bf16[8,72,1024]{2,1,0:T(8,128)(2,1)} %broadcast_in_dim.219), calls=%async_computation.2 | async-start | bytes 2359296 | tf_op jit(solution)/shard_map/all_to_all | solution.py:51
  117.0 35.7 %all-to-all-start.4 = ((bf16[8,64,2304]{2,1,0:T(8,128)(2,1)}), bf16[8,64,2304]{2,1,0:T(8,128)(2,1)}, u32[]{:S(2)}, u32[]{:S(2)}) async-start(bf16[8,64,2304]{2,1,0:T(8,128)(2,1)} %broadcast_in_dim.217), calls=%async_computation.4 | async-start | bytes 4718592 | tf_op jit(solution)/shard_map/all_to_all | solution.py:51
  121.5 27.9 %collective-permute-start.9 = (bf16[8,72,1024]{2,1,0:T(8,128)(2,1)}, bf16[8,72,1024]{2,1,0:T(8,128)(2,1)}, u32[]{:S(2)}, u32[]{:S(2)}) collective-permute-start(bf16[8,72,1024]{2,1,0:T(8,128)(2,1)} %all-to-all-done.2), channel_id=1, source_target_pairs={{0,8},{1,9},{2,10},{3,11},{4,12},{5,13},{6,14},{7,15},{8,0},{9,1},... | collective-permute-start | bytes 3538952 | tf_op jit(solution)/shard_map/ppermute | solution.py:47
  128.6 12.3 %collective-permute-start.6 = (bf16[192,1024]{1,0:T(8,128)(2,1)}, bf16[192,1024]{1,0:T(8,128)(2,1)}, u32[]{:S(2)}, u32[]{:S(2)}) collective-permute-start(bf16[192,1024]{1,0:T(8,128)(2,1)} %get-tuple-element.148), channel_id=1, source_target_pairs={{0,96},{1,97},{2,98},{3,99},{4,100},{5,101},{6,102},{7,103},{8,104... | collective-permute-start | bytes 1179656 | tf_op jit(solution)/shard_map/ppermute | solution.py:47
  154.2 33.6 %all-to-all-start.5 = ((bf16[8,64,2048]{2,1,0:T(8,128)(2,1)}), bf16[8,64,2048]{2,1,0:T(8,128)(2,1)}, u32[]{:S(2)}, u32[]{:S(2)}) async-start(bf16[8,64,2048]{2,1,0:T(8,128)(2,1)} %broadcast_in_dim.220), calls=%async_computation.5 | async-start | bytes 4194304 | tf_op jit(solution)/shard_map/all_to_all | solution.py:51
  197.1 15.8 %collective-permute-start.12 = (bf16[8,64,2304]{2,1,0:T(8,128)(2,1)}, bf16[8,64,2304]{2,1,0:T(8,128)(2,1)}, u32[]{:S(2)}, u32[]{:S(2)}) collective-permute-start(bf16[8,64,2304]{2,1,0:T(8,128)(2,1)} %dynamic-slice_bitcast_fusion), channel_id=1, source_target_pairs={{0,8},{1,9},{2,10},{3,11},{4,12},{5,13},{6,14},{7,15},{8,0},{9,1},... | collective-permute-start | bytes 7077896 | tf_op jit(solution)/shard_map/ppermute | solution.py:47
  198.3 21.5 %all-to-all-start.6 = ((bf16[8,72,1024]{2,1,0:T(8,128)(2,1)}), bf16[8,72,1024]{2,1,0:T(8,128)(2,1)}, u32[]{:S(2)}, u32[]{:S(2)}) async-start(bf16[8,72,1024]{2,1,0:T(8,128)(2,1)} %fusion.5), calls=%async_computation.6 | async-start | bytes 2359296 | tf_op jit(solution)/shard_map/all_to_all | solution.py:51
  219.8 34.8 %all-to-all-start.7 = ((bf16[8,64,2304]{2,1,0:T(8,128)(2,1)}), bf16[8,64,2304]{2,1,0:T(8,128)(2,1)}, u32[]{:S(2)}, u32[]{:S(2)}) async-start(bf16[8,64,2304]{2,1,0:T(8,128)(2,1)} %fusion), calls=%async_computation.7 | async-start | bytes 4718592 | tf_op jit(solution)/shard_map/all_to_all | solution.py:51
  254.6 19.7 %collective-permute-start.19 = (bf16[72,1024]{1,0:T(8,128)(2,1)S(1)}, bf16[72,1024]{1,0:T(8,128)(2,1)}, u32[]{:S(2)}, u32[]{:S(2)}) collective-permute-start(bf16[72,1024]{1,0:T(8,128)(2,1)S(1)} %reduce_sum.130), channel_id=1, source_target_pairs={{0,16},{1,17},{2,18},{3,19},{4,20},{5,21},{6,22},{7,23},{8,24},{9,... | collective-permute-start | bytes 442376 | tf_op jit(solution)/shard_map/ppermute | solution.py:47
  263.6 15.1 %collective-permute-start.17 = (bf16[8,64,1024]{2,1,0:T(8,128)(2,1)}, bf16[8,64,1024]{2,1,0:T(8,128)(2,1)}, u32[]{:S(2)}, u32[]{:S(2)}) collective-permute-start(bf16[8,64,1024]{2,1,0:T(8,128)(2,1)} %dynamic-slice_bitcast_fusion.2), channel_id=1, source_target_pairs={{0,8},{1,9},{2,10},{3,11},{4,12},{5,13},{6,14},{7,15},{8,0},{9,1},... | collective-permute-start | bytes 3145736 | tf_op jit(solution)/shard_map/ppermute | solution.py:47
  269.7 13.3 %all-to-all-start.8 = ((bf16[8,192,128]{2,1,0:T(8,128)(2,1)}), bf16[8,192,128]{2,1,0:T(8,128)(2,1)S(1)}, u32[]{:S(2)}, u32[]{:S(2)}) async-start(bf16[8,192,128]{2,1,0:T(8,128)(2,1)} %bitcast.225), calls=%async_computation.8 | async-start | bytes 786432 | tf_op jit(solution)/shard_map/all_to_all | solution.py:51
  283.0 28.2 %collective-permute-start.28 = (bf16[72,1024]{1,0:T(8,128)(2,1)}, bf16[72,1024]{1,0:T(8,128)(2,1)}, u32[]{:S(2)}, u32[]{:S(2)}) collective-permute-start(bf16[72,1024]{1,0:T(8,128)(2,1)} %add_convert_fusion.6), channel_id=1, source_target_pairs={{0,32},{1,33},{2,34},{3,35},{4,36},{5,37},{6,38},{7,39},{8,40},{9,... | collective-permute-start | bytes 442376 | tf_op jit(solution)/shard_map/ppermute | solution.py:47
  283.5 28.7 %collective-permute-start.29 = (bf16[72,1024]{1,0:T(8,128)(2,1)}, bf16[72,1024]{1,0:T(8,128)(2,1)}, u32[]{:S(2)}, u32[]{:S(2)}) collective-permute-start(bf16[72,1024]{1,0:T(8,128)(2,1)} %add_convert_fusion.6), channel_id=1, source_target_pairs={{0,96},{1,97},{2,98},{3,99},{4,100},{5,101},{6,102},{7,103},{8,104... | collective-permute-start | bytes 442376 | tf_op jit(solution)/shard_map/ppermute | solution.py:47
  286.0 37.5 %collective-permute-start.24 = (bf16[64,2304]{1,0:T(8,128)(2,1)}, bf16[64,2304]{1,0:T(8,128)(2,1)}, u32[]{:S(2)}, u32[]{:S(2)}) collective-permute-start(bf16[64,2304]{1,0:T(8,128)(2,1)} %add_convert_fusion.1), channel_id=1, source_target_pairs={{0,32},{1,33},{2,34},{3,35},{4,36},{5,37},{6,38},{7,39},{8,40},{9,... | collective-permute-start | bytes 884744 | tf_op jit(solution)/shard_map/ppermute | solution.py:47
  286.0 38.5 %collective-permute-start.25 = (bf16[64,2304]{1,0:T(8,128)(2,1)}, bf16[64,2304]{1,0:T(8,128)(2,1)}, u32[]{:S(2)}, u32[]{:S(2)}) collective-permute-start(bf16[64,2304]{1,0:T(8,128)(2,1)} %add_convert_fusion.1), channel_id=1, source_target_pairs={{0,96},{1,97},{2,98},{3,99},{4,100},{5,101},{6,102},{7,103},{8,104... | collective-permute-start | bytes 884744 | tf_op jit(solution)/shard_map/ppermute | solution.py:47
  288.9 27.9 %all-to-all-start.9 = ((bf16[8,64,1024]{2,1,0:T(8,128)(2,1)}), bf16[8,64,1024]{2,1,0:T(8,128)(2,1)}, u32[]{:S(2)}, u32[]{:S(2)}) async-start(bf16[8,64,1024]{2,1,0:T(8,128)(2,1)} %fusion.6), calls=%async_computation.9 | async-start | bytes 2097152 | tf_op jit(solution)/shard_map/all_to_all | solution.py:51
  316.8 18.7 %all-to-all-start.10 = ((bf16[8,192,256]{2,1,0:T(8,128)(2,1)}), bf16[8,192,256]{2,1,0:T(8,128)(2,1)S(1)}, u32[]{:S(2)}, u32[]{:S(2)}) async-start(bf16[8,192,256]{2,1,0:T(8,128)(2,1)} %bitcast.40), calls=%async_computation.10 | async-start | bytes 1572864 | tf_op jit(solution)/shard_map/all_to_all | solution.py:51
  335.5 18.1 %all-to-all-start.11 = ((bf16[8,144,256]{2,1,0:T(8,128)(2,1)}), bf16[8,144,256]{2,1,0:T(8,128)(2,1)S(1)}, u32[]{:S(2)}, u32[]{:S(2)}) async-start(bf16[8,144,256]{2,1,0:T(8,128)(2,1)} %maximum_maximum_fusion), calls=%async_computation.11 | async-start | bytes 1179648 | tf_op jit(solution)/shard_map/all_to_all | solution.py:51
  344.2 26.2 %collective-permute-start.21 = (bf16[192,1024]{1,0:T(8,128)(2,1)}, bf16[192,1024]{1,0:T(8,128)(2,1)S(1)}, u32[]{:S(2)}, u32[]{:S(2)}) collective-permute-start(bf16[192,1024]{1,0:T(8,128)(2,1)} %pad_maximum_fusion.7), channel_id=1, source_target_pairs={{0,32},{1,33},{2,34},{3,35},{4,36},{5,37},{6,38},{7,39},{8,40},{9,... | collective-permute-start | bytes 1179656 | tf_op jit(solution)/shard_map/ppermute | solution.py:47
  345.0 25.5 %collective-permute-start.23 = (bf16[192,1024]{1,0:T(8,128)(2,1)}, bf16[192,1024]{1,0:T(8,128)(2,1)}, u32[]{:S(2)}, u32[]{:S(2)}) collective-permute-start(bf16[192,1024]{1,0:T(8,128)(2,1)} %pad_maximum_fusion.8), channel_id=1, source_target_pairs={{0,96},{1,97},{2,98},{3,99},{4,100},{5,101},{6,102},{7,103},{8,104... | collective-permute-start | bytes 1179656 | tf_op jit(solution)/shard_map/ppermute | solution.py:47
  347.7 18.4 %collective-permute-start.32 = (bf16[8,64,2048]{2,1,0:T(8,128)(2,1)}, bf16[8,64,2048]{2,1,0:T(8,128)(2,1)}, u32[]{:S(2)}, u32[]{:S(2)}) collective-permute-start(bf16[8,64,2048]{2,1,0:T(8,128)(2,1)} %all-to-all-done.5), channel_id=1, source_target_pairs={{0,8},{1,9},{2,10},{3,11},{4,12},{5,13},{6,14},{7,15},{8,0},{9,1},... | collective-permute-start | bytes 6291464 | tf_op jit(solution)/shard_map/ppermute | solution.py:47
  357.9 21.5 %all-to-all-start.12 = ((bf16[16,104,256]{2,1,0:T(8,128)(2,1)}), bf16[16,104,256]{2,1,0:T(8,128)(2,1)S(1)}, u32[]{:S(2)}, u32[]{:S(2)}) async-start(bf16[16,104,256]{2,1,0:T(8,128)(2,1)} %fusion.25), calls=%async_computation.12 | async-start | bytes 1703936 | tf_op jit(solution)/shard_map/all_to_all | solution.py:538
  380.5 18.0 %all-to-all-start.13 = ((bf16[16,104,256]{2,1,0:T(8,128)(2,1)}), bf16[16,104,256]{2,1,0:T(8,128)(2,1)S(1)}, u32[]{:S(2)}, u32[]{:S(2)}) async-start(bf16[16,104,256]{2,1,0:T(8,128)(2,1)} %broadcast_in_dim.247), calls=%async_computation.13 | async-start | bytes 1703936 | tf_op jit(solution)/shard_map/all_to_all | solution.py:541
  386.9 24.1 %collective-permute-start.34 = (bf16[4,72,1024]{2,1,0:T(8,128)(2,1)S(1)}, bf16[4,72,1024]{2,1,0:T(8,128)(2,1)S(1)}, u32[]{:S(2)}, u32[]{:S(2)}) collective-permute-start(bf16[4,72,1024]{2,1,0:T(8,128)(2,1)S(1)} %pad_maximum_fusion.3.down_mine_ref), channel_id=1, source_target_pairs={{0,8},{1,9},{2,10},{3,11},{4,12},{5,13},{6,14},{7,15},{8,0},{9,1},... | collective-permute-start | bytes 1769480 | tf_op jit(solution)/shard_map/ppermute | solution.py:47
  388.5 22.6 %collective-permute-start.33 = (bf16[4,64,2304]{2,1,0:T(8,128)(2,1)S(1)}, bf16[4,64,2304]{2,1,0:T(8,128)(2,1)}, u32[]{:S(2)}, u32[]{:S(2)}) collective-permute-start(bf16[4,64,2304]{2,1,0:T(8,128)(2,1)S(1)} %pad_maximum_fusion.1.mine_ref), channel_id=1, source_target_pairs={{0,8},{1,9},{2,10},{3,11},{4,12},{5,13},{6,14},{7,15},{8,0},{9,1},... | collective-permute-start | bytes 3538952 | tf_op jit(solution)/shard_map/ppermute | solution.py:47
  (58 other events, 388.0 us)
Sparse Core Ops, SparseCore 0:
  10.3 74.2 all-gather.2
